TPU v7x, 32 devices: a whole 2x2x4 slice. The times are simulated.
32 devices in a mesh: rep: 4 (over z), fsdp: 8 (over y, x, core).
Axes of the slice: x: 2, y: 2, z: 4, core: 2. Of those that a mesh axis runs over, the one named last changes fastest.
Arguments:
- tokens: bfloat16 [32, 1024, 768], P(('rep', 'fsdp')), may hold values from -6 to 6
- segments: int32 [32, 1024], P(('rep', 'fsdp')), may hold values from 0 to 5, never falling along the last dimension, each value on 1 to 800 neighbouring positions
- w_in: bfloat16 [2, 768, 3328], P(None, 'fsdp'), may hold values from -0.21875 to 0.21875
- w_dt: bfloat16 [2, 768, 24], P(None, 'fsdp'), may hold values from -0.21875 to 0.21875
- w_out: bfloat16 [2, 1536, 768], P(None, 'fsdp'), may hold values from -0.15625 to 0.15625
- conv_w: bfloat16 [2, 4, 1792], P(None, None, 'fsdp'), may hold values from -3 to 3
- conv_b: bfloat16 [2, 1792], P(None, 'fsdp'), may hold values from -0.5 to 0.5
- norm_in: bfloat16 [2, 768], P(None, 'fsdp'), may hold values from 0.5 to 1.5
- norm_gate: bfloat16 [2, 1536], P(None, 'fsdp'), may hold values from 0.5 to 1.5
- dt_bias: float32 [2, 24], replicated, may hold values from -3 to -1
- a_log: float32 [2, 24], replicated, may hold values from -3 to 1.5
- d_skip: float32 [2, 24], replicated, may hold values from 0.5 to 1.5
- cotangent: bfloat16 [32, 1024, 768], P(('rep', 'fsdp')), may hold values from -6 to 6
Outputs:
- mixed: bfloat16 [32, 1024, 768], P(('rep', 'fsdp'))
- grad_tokens: float32 [32, 1024, 768], P(('rep', 'fsdp'))
- grad_w_in: float32 [2, 768, 3328], P(None, 'fsdp')
- grad_w_dt: float32 [2, 768, 24], P(None, 'fsdp')
- grad_w_out: float32 [2, 1536, 768], P(None, 'fsdp')
- grad_conv_w: float32 [2, 4, 1792], P(None, None, 'fsdp')
- grad_conv_b: float32 [2, 1792], P(None, 'fsdp')
- grad_norm_in: float32 [2, 768], P(None, 'fsdp')
- grad_norm_gate: float32 [2, 1536], P(None, 'fsdp')
- grad_dt_bias: float32 [2, 24], replicated
- grad_a_log: float32 [2, 24], replicated
- grad_d_skip: float32 [2, 24], replicated
Inputs may be any that keep to these rules, and one draw needn't show every extreme that they name: `segments`: in each sequence the document numbers run from 0 to 5 without falling; each document has 1 to 800 tokens and one has exactly 800.
All inputs are finite; a program needn't handle non-finite values.
Results may differ from a plain program's by a relative error of at most 0.013.
Values may be sent and summed in bfloat16 or wider, within the bound.
A program may use at most 320 MiB of HBM per device.

v0:
```python
import jax
import jax.numpy as jnp
from jax import lax
from jax.sharding import PartitionSpec as P

SPAN = 256


EPSILON = 1e-05
HIGHEST = lax.Precision.HIGHEST


def normalize(values, weight):
    return values * lax.rsqrt(jnp.mean(values * values, axis=-1, keepdims=True) + EPSILON) * weight


def block_step(carry_state, inputs):
    values_block, b_block, c_block, dt_block, rate_block, seg_block, carried_block = inputs
    cumulative = jnp.cumsum(rate_block, axis=0)
    position = jnp.arange(seg_block.shape[0])
    lower_tri = position[:, None] >= position[None, :]
    same_doc = (lower_tri & (seg_block[:, None] == seg_block[None, :])).astype(rate_block.dtype)
    by_head = cumulative.T
    log_decay = by_head[:, :, None] - by_head[:, None, :]
    decay_mat = jnp.exp(jnp.where(same_doc[None] > 0, log_decay, 0.0)) * same_doc[None]
    intersection = jnp.dot(c_block, b_block.T, precision=HIGHEST)
    mixing = decay_mat * intersection[None] * dt_block.T[:, None, :]
    inside = jnp.einsum("hij,jhp->ihp", mixing, values_block, precision=HIGHEST)
    outside = jnp.einsum("in,hpn->ihp", c_block, carry_state, precision=HIGHEST)
    outside = outside * (carried_block[:, None] * jnp.exp(cumulative))[:, :, None]
    last_rate = cumulative[-1]
    weight_last = (
        jnp.exp(last_rate[None, :] - cumulative)
        * (seg_block == seg_block[-1]).astype(rate_block.dtype)[:, None]
        * dt_block
    )
    new_state = carry_state * (carried_block[-1] * jnp.exp(last_rate))[:, None, None]
    new_state = new_state + jnp.einsum(
        "jh,jhp,jn->hpn", weight_last, values_block, b_block, precision=HIGHEST
    )
    return (new_state, inside + outside)


def mixer(
    projected, dt_raw, segment, conv_weight, conv_bias, gate_gain, bias_dt, log_rate, skip_gain
):
    length = projected.shape[0]
    inner = gate_gain.shape[0]
    heads = bias_dt.shape[0]
    headdim = inner // heads
    state_size = (projected.shape[1] - 2 * inner) // 2
    kernel = conv_weight.shape[0]
    gate_part = projected[:, :inner]
    conv_in = projected[:, inner:]
    summed = conv_bias[None, :] + conv_weight[kernel - 1][None, :] * conv_in
    for shift_by in range(1, kernel):
        shifted = jnp.pad(conv_in, ((shift_by, 0), (0, 0)))[:length]
        shifted_seg = jnp.pad(segment, (shift_by, 0), constant_values=-1)[:length]
        keeping = (shifted_seg == segment).astype(projected.dtype)
        summed = summed + conv_weight[kernel - 1 - shift_by][None, :] * shifted * keeping[:, None]
    conv_out = jax.nn.silu(summed)
    values = conv_out[:, :inner].reshape(length, heads, headdim)
    b_input = conv_out[:, inner : inner + state_size]
    c_output = conv_out[:, inner + state_size :]
    step_dt = jax.nn.softplus(dt_raw + bias_dt[None, :])
    decay_rate = -jnp.exp(log_rate)[None, :] * step_dt
    blocks = length // SPAN
    seg_blocks = segment.reshape(blocks, SPAN)
    before = jnp.concatenate([jnp.full((1,), -1, jnp.int32), seg_blocks[:-1, -1]])
    carried = (seg_blocks == before[:, None]).astype(projected.dtype)
    scanned = (
        values.reshape(blocks, SPAN, heads, headdim),
        b_input.reshape(blocks, SPAN, state_size),
        c_output.reshape(blocks, SPAN, state_size),
        step_dt.reshape(blocks, SPAN, heads),
        decay_rate.reshape(blocks, SPAN, heads),
        seg_blocks,
        carried,
    )
    initial = jnp.zeros((heads, headdim, state_size), projected.dtype)
    unused, outputs = lax.scan(jax.checkpoint(block_step), initial, scanned)
    result = outputs.reshape(length, heads, headdim) + skip_gain[None, :, None] * values
    result = result.reshape(length, inner) * jax.nn.silu(gate_part)
    return normalize(result, gate_gain[None, :])


def contract_rows(left, right):
    return lax.dot_general(
        left, right, (((0,), (0,)), ((), ())), preferred_element_type=jnp.float32
    )


def contract_cols(left, right):
    return lax.dot_general(
        left, right, (((1,), (1,)), ((), ())), preferred_element_type=jnp.float32
    )


def fetch_forward(w_in, w_dt, w_out, conv_w, conv_b, norm_in, norm_gate, layer_index):
    return (
        lax.all_gather(w_in[layer_index], "fsdp", axis=0, tiled=True),
        lax.all_gather(w_dt[layer_index], "fsdp", axis=0, tiled=True),
        lax.all_gather(w_out[layer_index], "fsdp", axis=0, tiled=True),
        lax.all_gather(conv_w[layer_index], "fsdp", axis=1, tiled=True),
        lax.all_gather(conv_b[layer_index], "fsdp", axis=0, tiled=True),
        lax.all_gather(norm_in[layer_index], "fsdp", axis=0, tiled=True),
        lax.all_gather(norm_gate[layer_index], "fsdp", axis=0, tiled=True),
    )


def fetch_backward(w_in, w_dt, w_out, conv_w, conv_b, norm_in, norm_gate, layer_index):
    return (
        lax.all_gather(w_in[layer_index], "fsdp", axis=0, tiled=True),
        lax.all_gather(w_dt[layer_index], "fsdp", axis=0, tiled=True),
        lax.all_gather(w_out[layer_index], "fsdp", axis=0, tiled=True),
        lax.all_gather(conv_w[layer_index], "fsdp", axis=1, tiled=True),
        lax.all_gather(conv_b[layer_index], "fsdp", axis=0, tiled=True),
        lax.all_gather(norm_in[layer_index], "fsdp", axis=0, tiled=True),
        lax.all_gather(norm_gate[layer_index], "fsdp", axis=0, tiled=True),
    )


def layer_forward(hidden, gathered, segment, bias_dt, log_rate, skip_gain):
    in_weights, dt_weights, out_weights, conv_weight, conv_bias, norm_gain, gate_gain = gathered
    normed, norm_back = jax.vjp(normalize, hidden, norm_gain.astype(jnp.float32))
    normed_low = normed.astype(jnp.bfloat16)
    projected = jnp.dot(normed_low, in_weights, preferred_element_type=jnp.float32)
    dt_raw = jnp.dot(normed_low, dt_weights, preferred_element_type=jnp.float32)

    def mixing_fn(proj_in, raw_in, taps_in, shift_in, gate_in, bias_in, rate_in, skip_in):
        return mixer(
            proj_in, raw_in, segment, taps_in, shift_in, gate_in, bias_in, rate_in, skip_in
        )

    gated, mixer_back = jax.vjp(
        mixing_fn,
        projected,
        dt_raw,
        conv_weight.astype(jnp.float32),
        conv_bias.astype(jnp.float32),
        gate_gain.astype(jnp.float32),
        bias_dt,
        log_rate,
        skip_gain,
    )
    gated_low = gated.astype(jnp.bfloat16)
    output = hidden + jnp.dot(gated_low, out_weights, preferred_element_type=jnp.float32)
    return (output, (norm_back, normed_low, mixer_back, gated_low))


def layer_backward(grad_hidden, gathered, saved):
    in_weights, dt_weights, out_weights = (gathered[0], gathered[1], gathered[2])
    norm_back, normed_low, mixer_back, gated_low = saved
    grad_low = grad_hidden.astype(jnp.bfloat16)
    grad_wout = contract_rows(gated_low, grad_low)
    grad_gated = contract_cols(grad_low, out_weights)
    grad_proj, grad_raw, grad_taps, grad_shift, grad_gate, grad_bias, grad_rate, grad_skip = (
        mixer_back(grad_gated)
    )
    proj_low = grad_proj.astype(jnp.bfloat16)
    raw_low = grad_raw.astype(jnp.bfloat16)
    grad_win = contract_rows(normed_low, proj_low)
    grad_wdt = contract_rows(normed_low, raw_low)
    grad_normed = contract_cols(proj_low, in_weights) + contract_cols(raw_low, dt_weights)
    grad_input, grad_gain = norm_back(grad_normed)
    matrices = (grad_win, grad_wdt, grad_wout, grad_taps, grad_shift, grad_gain, grad_gate)
    return (grad_hidden + grad_input, matrices, (grad_bias, grad_rate, grad_skip))


def shards(
    tokens,
    segments,
    w_in,
    w_dt,
    w_out,
    conv_w,
    conv_b,
    norm_in,
    norm_gate,
    dt_bias,
    a_log,
    d_skip,
    cotangent,
):
    segment = segments[0]
    hidden = tokens[0].astype(jnp.float32)
    layer_count = w_in.shape[0]
    gathered_list = []
    saved_list = []
    for layer_index in range(layer_count):
        gathered = fetch_forward(w_in, w_dt, w_out, conv_w, conv_b, norm_in, norm_gate, layer_index)
        hidden, saved = layer_forward(
            hidden, gathered, segment, dt_bias[layer_index], a_log[layer_index], d_skip[layer_index]
        )
        gathered_list.append(gathered)
        saved_list.append(saved)
    grad_hidden = cotangent[0].astype(jnp.float32)
    owned_list = [None] * layer_count
    head_list = [None] * layer_count
    for layer_index in reversed(range(layer_count)):
        gathered = fetch_backward(
            w_in, w_dt, w_out, conv_w, conv_b, norm_in, norm_gate, layer_index
        )
        grad_hidden, matrices, head_terms = layer_backward(
            grad_hidden, gathered, saved_list[layer_index]
        )
        owned = (
            lax.psum_scatter(matrices[0], "fsdp", scatter_dimension=0, tiled=True),
            lax.psum_scatter(matrices[1], "fsdp", scatter_dimension=0, tiled=True),
            lax.psum_scatter(matrices[2], "fsdp", scatter_dimension=0, tiled=True),
            lax.psum_scatter(matrices[3], "fsdp", scatter_dimension=1, tiled=True),
            lax.psum_scatter(matrices[4], "fsdp", scatter_dimension=0, tiled=True),
            lax.psum_scatter(matrices[5], "fsdp", scatter_dimension=0, tiled=True),
            lax.psum_scatter(matrices[6], "fsdp", scatter_dimension=0, tiled=True),
        )
        owned = (
            lax.psum(owned[0].astype(jnp.bfloat16), "rep").astype(jnp.float32),
            lax.psum(owned[1].astype(jnp.bfloat16), "rep").astype(jnp.float32),
            lax.psum(owned[2].astype(jnp.bfloat16), "rep").astype(jnp.float32),
            lax.psum(owned[3].astype(jnp.bfloat16), "rep").astype(jnp.float32),
            lax.psum(owned[4].astype(jnp.bfloat16), "rep").astype(jnp.float32),
            lax.psum(owned[5].astype(jnp.bfloat16), "rep").astype(jnp.float32),
            lax.psum(owned[6].astype(jnp.bfloat16), "rep").astype(jnp.float32),
        )
        owned_list[layer_index] = owned
        head_list[layer_index] = head_terms
    stacked = tuple(
        (
            jnp.stack([owned_list[layer_index][member] for layer_index in range(layer_count)])
            for member in range(7)
        )
    )
    bias_stack = jnp.stack([head_list[layer_index][0] for layer_index in range(layer_count)])
    rate_stack = jnp.stack([head_list[layer_index][1] for layer_index in range(layer_count)])
    skip_stack = jnp.stack([head_list[layer_index][2] for layer_index in range(layer_count)])
    head_sums = lax.psum((bias_stack, rate_stack, skip_stack), ("rep", "fsdp"))
    return (
        hidden.astype(jnp.bfloat16)[None],
        grad_hidden[None],
        stacked[0],
        stacked[1],
        stacked[2],
        stacked[3],
        stacked[4],
        stacked[5],
        stacked[6],
        head_sums[0],
        head_sums[1],
        head_sums[2],
    )


def solution(mesh):
    placed = (
        P(("rep", "fsdp"), None, None),
        P(("rep", "fsdp"), None),
        P(None, "fsdp", None),
        P(None, "fsdp", None),
        P(None, "fsdp", None),
        P(None, None, "fsdp"),
        P(None, "fsdp"),
        P(None, "fsdp"),
        P(None, "fsdp"),
        P(),
        P(),
        P(),
        P(("rep", "fsdp"), None, None),
    )
    return jax.shard_map(
        shards,
        mesh=mesh,
        in_specs=placed,
        out_specs=(
            P(("rep", "fsdp"), None, None),
            P(("rep", "fsdp"), None, None),
            P(None, "fsdp", None),
            P(None, "fsdp", None),
            P(None, "fsdp", None),
            P(None, None, "fsdp"),
            P(None, "fsdp"),
            P(None, "fsdp"),
            P(None, "fsdp"),
            P(),
            P(),
            P(),
        ),
        check_vma=False,
    )
```

profile of v0, /device:TPU:0, one launch (start us, length us, event | category | flops | bytes accessed | tf_op | source)
XLA Modules:
  0.0 1931.9 jit_solution(16943706958026840383)
XLA Ops:
  20.0 26.6 %all-reduce.49 = (bf16[768]{0:T(1024)(128)(2,1)S(1)}, bf16[1792]{0:T(1024)(128)(2,1)S(1)}, bf16[1536]{0:T(1024)(128)(2,1)}, bf16[768]{0:T(1024)(128)(2,1)}, bf16...) all-reduce(bf16[768]{0:T(1024)(128)(2,1)S(1)} %dynamic-update-slice, ...), channel_id=2, replica_groups=mesh['rep'=4,'fsdp'=8] {'fsdp'}, use_global_device_ids=true, to_apply=%add.35 | all-reduce | flops 8192 | bytes 32768
  61.7 38.1 %slice_reduce_fusion.15 = (f32[1792]{0:T(1024)}, f32[1792]{0:T(1024)}, f32[1792]{0:T(1024)}, f32[1792]{0:T(1024)}) fusion(f32[1,4,1792]{1,0,2:T(1,128)S(1)} %convert_element_type.289), kind=kLoop, calls=%fused_computation.419 | loop fusion | bytes 57344 | tf_op jit(solution)/shard_map/jvp()/slice | solution.py:55
  135.4 38.2 %slice_reduce_fusion.11 = (f32[1792]{0:T(1024)}, f32[1792]{0:T(1024)}, f32[1792]{0:T(1024)}, f32[1792]{0:T(1024)}) fusion(f32[1,4,1792]{1,0,2:T(1,128)S(1)} %convert_element_type.293), kind=kLoop, calls=%fused_computation.415 | loop fusion | bytes 57344 | tf_op jit(solution)/shard_map/jvp()/slice | solution.py:55
  243.1 92.5 %while.82 = (s32[]{:T(128)}, f32[24,64,128]{2,1,0:T(8,128)S(1)}, f32[4,256,24,64]{1,3,2,0:T(8,128)}, f32[4,24,64,128]{3,2,1,0:T(8,128)}, f32[4,256]{1,0:T(4,128)...) while((s32[]{:T(128)}, f32[24,64,128]{2,1,0:T(8,128)S(1)}, ...), condition=%wide.region_4.6_spmd.clone, body=%wide.region_1.5_spmd.clone.sunk | while | flops 2527754752 | bytes 14008185 | solution.py:81
  345.4 11.1 reshape.1213
  429.6 85.3 %while.83 = (s32[]{:T(128)}, f32[24,64,128]{2,1,0:T(8,128)S(1)}, f32[4,256,24,64]{1,3,2,0:T(8,128)}, f32[4,24,64,128]{3,2,1,0:T(8,128)}, f32[4,256]{1,0:T(4,128)...) while((s32[]{:T(128)}, f32[24,64,128]{2,1,0:T(8,128)S(1)}, ...), condition=%wide.region_10.12_spmd.clone, body=%wide.region_7.11_spmd.clone.sunk | while | flops 2527754752 | bytes 14008601 | solution.py:81
  525.1 11.1 reshape.1214
  557.5 13.5 multiply_reduce_fusion.18
  597.4 347.1 %while.84 = (s32[]{:T(128)}, f32[24,64,128]{2,1,0:T(8,128)}, f32[4,256,24,64]{1,3,2,0:T(8,128)}, f32[4,256,128]{2,1,0:T(8,128)}, f32[4,256,128]{2,1,0:T(8,128)},...) while((s32[]{:T(128)}, f32[24,64,128]{2,1,0:T(8,128)}, ...), condition=%wide.region_25.27_spmd.clone, body=%wide.region_13.26_spmd.clone.sunk | while | flops 5775804928 | bytes 39969528 | solution.py:81
  627.2 12.3 fusion.449
  714.1 12.3 fusion.449
  801.0 12.3 fusion.449
  887.9 12.3 fusion.449
  956.3 11.2 reshape.1216
  1027.8 14.6 multiply_reduce_fusion.19
  1068.8 347.6 %while.85 = (s32[]{:T(128)}, f32[24,64,128]{2,1,0:T(8,128)}, f32[4,256,24,64]{1,3,2,0:T(8,128)}, f32[4,256,128]{2,1,0:T(8,128)}, f32[4,256,128]{2,1,0:T(8,128)},...) while((s32[]{:T(128)}, f32[24,64,128]{2,1,0:T(8,128)}, ...), condition=%wide.region_40.42_spmd.clone, body=%wide.region_28.41_spmd.clone.sunk | while | flops 5775804928 | bytes 39969528 | solution.py:81
  1098.9 12.4 fusion.476
  1185.8 12.4 fusion.476
  1272.8 12.4 fusion.476
  1359.7 12.4 fusion.476
  1426.2 11.2 reshape.1218
  1454.3 35.6 %multiply_reduce_fusion.13 = (f32[1792]{0:T(1024)S(1)}, f32[1792]{0:T(1024)S(1)}, f32[1792]{0:T(1024)S(1)}, f32[1792]{0:T(1024)S(1)}, f32[1792]{0:T(1024)S(1)}, ...) fusion(f32[1024,1792]{1,0:T(8,128)} %copy-done.2, ...), kind=kLoop, calls=%fused_computation.321 | loop fusion | flops 64207360 | bytes 58804224 | tf_op jit(solution)/shard_map/transpose(jvp())/reduce_sum | solution.py:60
  1505.3 14.4 fusion.244
  1521.1 14.1 fusion.243
  1564.9 25.3 %all-reduce.48 = (bf16[1792]{0:T(1024)(128)(2,1)S(1)}, bf16[1792]{0:T(1024)(128)(2,1)S(1)}, bf16[768]{0:T(1024)(128)(2,1)S(1)}, bf16[768]{0:T(1024)(128)(2,1)S(1...) all-reduce(f32[1792]{0:T(1024)S(1)} %get-tuple-element.1639, ...), channel_id=25, replica_groups=mesh['rep'=4,'fsdp'=8] {'fsdp'}, use_global_device_ids=true, to_apply=%region_70.72.clone | all-reduce | flops 8192 | bytes 49152
  1603.6 82.0 %reduce-scatter.19.cloned.1.call-done = f32[96,3328]{1,0:T(8,128)} async-done(((f32[768,3328]{1,0:T(8,128)}), f32[96,3328]{1,0:T(8,128)}) %reduce-scatter.19.cloned.1.call-update) | async-done | bytes 1277968 | tf_op jit(solution)/shard_map/reduce_scatter | solution.py:208
  1698.4 39.4 %all-reduce.47 = (f32[2,24]{1,0:T(2,128)}, f32[2,24]{1,0:T(2,128)}, f32[2,24]{1,0:T(2,128)}) all-reduce(f32[2,24]{1,0:T(2,128)S(1)} %pad_maximum_fusion, f32[2,24]{1,0:T(2,128)S(1)} %pad_maximum_fusion.1, f32[2,24]{1,0:T(2,128)S(1)} %pad_maximum_fusion.2), channel_id=1, replica_groups=mesh['rep'=4,'fsdp'=8] {'rep','fsdp'}, use_global_device_ids=true, to_apply=%region_86.88 | all-reduce | flops 144 | bytes 1152 | tf_op jit(solution)/shard_map/psum | solution.py:236
  1738.9 24.6 %reduce-scatter.31.cloned.1.call-done = f32[224,4]{1,0:T(8,128)} async-done(((f32[1792,4]{1,0:T(8,128)}), f32[224,4]{1,0:T(8,128)}) %reduce-scatter.31.cloned.1.call-update) | async-done | bytes 3600
  1764.4 36.0 %reduce-scatter.25.cloned.1.call-done = f32[96,24]{1,0:T(8,128)} async-done(((f32[768,24]{1,0:T(8,128)}), f32[96,24]{1,0:T(8,128)}) %reduce-scatter.25.cloned.1.call-update) | async-done | bytes 9232
  1801.3 35.9 %reduce-scatter.27.cloned.1.call-done = f32[96,24]{1,0:T(8,128)} async-done(((f32[768,24]{1,0:T(8,128)}), f32[96,24]{1,0:T(8,128)}) %reduce-scatter.27.cloned.1.call-update) | async-done | bytes 9232
  1838.0 19.7 %all-reduce.50 = (bf16[1,96,24]{1,2,0:T(8,128)(2,1)S(1)}, bf16[1,96,24]{1,2,0:T(8,128)(2,1)S(1)}, bf16[1,4,224]{2,1,0:T(4,128)(2,1)S(1)}, bf16[1,4,224]{2,1,0:T(...) all-reduce(bf16[1,96,24]{1,2,0:T(8,128)(2,1)S(1)} %bitcast.882, ...), channel_id=1, replica_groups=mesh['rep'=4,'fsdp'=8] {'rep'}, use_global_device_ids=true, to_apply=%region_49.51 | all-reduce | flops 7424 | bytes 29696 | tf_op jit(solution)/shard_map/psum | solution.py:218
  1860.7 59.4 %all-reduce.54.cloned.1.call-done = (bf16[1,96,3328]{2,1,0:T(8,128)(2,1)}, bf16[1,96,3328]{2,1,0:T(8,128)(2,1)}, bf16[1,192,768]{2,1,0:T(8,128)(2,1)}, bf16[1,192,768]{2,1,0:T(8,128)(2,1)}) async-done(((bf16[1,96,3328]{2,1,0:T(8,128)(2,1)}, bf16[1,96,3328]{2,1,0:T(8,128)(2,1)}, bf16[1,192,768]{2,1,0:T(8,128)(2,1)}, bf16[1,192,768]{2,1,0:T(8,128)(2,1)}), (bf16[1,96,3328]{2,1,0:T(8,128)(2,1)}, ...) | async-done | bytes 1867792 | tf_op jit(solution)/shard_map/psum | solution.py:217
  (1088 shorter events, 1248.2 us)
Async XLA Ops:
  7.2 42.2 %copy-start.99 = (s32[1,1024]{1,0:T(1,128)S(1)}, s32[1,1024]{1,0:T(1,128)}, u32[]{:S(2)}) copy-start(s32[1,1024]{1,0:T(1,128)} %param.23) | copy-start | bytes 12292
  7.2 42.9 %copy-start.105 = (bf16[2,4,224]{2,1,0:T(4,128)(2,1)S(1)}, bf16[2,4,224]{2,1,0:T(4,128)(2,1)}, u32[]{:S(2)}) copy-start(bf16[2,4,224]{2,1,0:T(4,128)(2,1)} %param.27) | copy-start | bytes 10756
  7.2 183.0 %all-gather.19.cloned.1.call-start = ((), (), s32[]{:S(2)}) async-start(), calls=%async_computation.12 | async-start | bytes 5750784 | tf_op jit(solution)/shard_map/all_gather | solution.py:101
  9.7 357.3 %all-gather.21.cloned.1.call-start = ((), (), s32[]{:S(2)}) async-start(), calls=%async_computation.13 | async-start | bytes 2654208 | tf_op jit(solution)/shard_map/all_gather | solution.py:103
  11.6 88.2 %copy-start.100 = (bf16[2,96,24]{1,2,0:T(8,128)(2,1)S(1)}, bf16[2,96,24]{1,2,0:T(8,128)(2,1)}, u32[]{:S(2)}) copy-start(bf16[2,96,24]{1,2,0:T(8,128)(2,1)} %param.25) | copy-start | bytes 27652
  11.7 363.7 %all-gather.23.cloned.1.call-start = ((), (), s32[]{:S(2)}) async-start(), calls=%async_computation.14 | async-start | bytes 5750784 | tf_op jit(solution)/shard_map/all_gather | solution.py:101
  12.4 534.4 %all-gather.25.cloned.1.call-start = ((), (), s32[]{:S(2)}) async-start(), calls=%async_computation.15 | async-start | bytes 2654208 | tf_op jit(solution)/shard_map/all_gather | solution.py:103
  13.0 98.8 %copy-start.106 = (f32[2,24]{1,0:T(2,128)S(1)}, f32[2,24]{1,0:T(2,128)}, u32[]{:S(2)}) copy-start(f32[2,24]{1,0:T(2,128)} %param.32) | copy-start | bytes 580
  13.0 1581.6 %reduce-scatter.21.cloned.1.call-start = ((), (), s32[]{:S(2)}) async-start(), calls=%async_computation.10 | async-start | bytes 5308416 | tf_op jit(solution)/shard_map/reduce_scatter | solution.py:210
  46.5 143.6 %copy-start.28 = (f32[768]{0:T(1024)}, f32[768]{0:T(1024)S(1)}, u32[]{:S(2)}) copy-start(f32[768]{0:T(1024)S(1)} %convert_element_type.295) | copy-start | bytes 9220
  48.3 141.9 %copy-start.8 = (bf16[1,1024,768]{1,2,0:T(8,128)(2,1)}, bf16[1,1024,768]{1,2,0:T(8,128)(2,1)S(1)}, u32[]{:S(2)}) copy-start(bf16[1,1024,768]{1,2,0:T(8,128)(2,1)S(1)} %copy.466) | copy-start | bytes 4718596
  48.7 141.5 %copy-start.30 = (f32[1024]{0:T(1024)}, f32[1024]{0:T(1024)S(1)}, u32[]{:S(2)}) copy-start(f32[1024]{0:T(1024)S(1)} %fusion.270) | copy-start | bytes 12292
  111.7 61.9 %copy-start.90 = (bf16[1,96,24]{1,2,0:T(8,128)(2,1)S(1)}, bf16[1,96,24]{1,2,0:T(8,128)(2,1)}, u32[]{:S(2)}) copy-start(bf16[1,96,24]{1,2,0:T(8,128)(2,1)} %get-tuple-element.1874) | copy-start | bytes 13828
  375.4 45.9 %copy-start.15 = (bf16[1024,768]{0,1:T(8,128)(2,1)}, bf16[1024,768]{0,1:T(8,128)(2,1)S(1)}, u32[]{:S(2)}) copy-start(bf16[1024,768]{0,1:T(8,128)(2,1)S(1)} %multiply_convert_fusion.2) | copy-start | bytes 4718596
  536.2 21.2 %slice-start.2 = ((s8[7340032]{0:T(1024)(128)(4,1)}), s8[3145728]{0:T(1024)(128)(4,1)S(1)}, s32[]{:S(2)}) async-start(s8[7340032]{0:T(1024)(128)(4,1)} %bitcast.827), calls=%async_computation.23 | async-start | bytes 6291456
  714.1 15.3 copy-start.54
  801.0 15.3 copy-start.54
  887.9 15.3 copy-start.54
  990.6 18.8 copy-start.32
  1062.2 534.3 %reduce-scatter.23.cloned.1.call-start = ((), (), s32[]{:S(2)}) async-start(), calls=%async_computation.11 | async-start | bytes 5308416 | tf_op jit(solution)/shard_map/reduce_scatter | solution.py:210
  1454.2 147.2 %reduce-scatter.17.cloned.1.call-start = ((), (), s32[]{:S(2)}) async-start(), calls=%async_computation.8 | async-start | bytes 11501568 | tf_op jit(solution)/shard_map/reduce_scatter | solution.py:208
  1454.3 35.7 %copy-start.61 = (f32[1792]{0:T(1024)S(1)}, f32[1792]{0:T(1024)}, u32[]{:S(2)}) copy-start(f32[1792]{0:T(1024)} %get-tuple-element.1651) | copy-start | bytes 21508
  1454.3 35.7 %copy-start.63 = (f32[1792]{0:T(1024)S(1)}, f32[1792]{0:T(1024)}, u32[]{:S(2)}) copy-start(f32[1792]{0:T(1024)} %get-tuple-element.1652) | copy-start | bytes 21508
  1454.3 35.7 %copy-start.65 = (f32[1792]{0:T(1024)S(1)}, f32[1792]{0:T(1024)}, u32[]{:S(2)}) copy-start(f32[1792]{0:T(1024)} %get-tuple-element.1653) | copy-start | bytes 21508
  1519.8 165.8 %reduce-scatter.19.cloned.1.call-start = ((), (), s32[]{:S(2)}) async-start(), calls=%async_computation.9 | async-start | bytes 11501568 | tf_op jit(solution)/shard_map/reduce_scatter | solution.py:208
  1535.2 202.7 %reduce-scatter.29.cloned.1.call-start = ((), (), s32[]{:S(2)}) async-start(), calls=%async_computation.18 | async-start | bytes 1032192
  1555.9 207.6 %reduce-scatter.31.cloned.1.call-start = ((), (), s32[]{:S(2)}) async-start(), calls=%async_computation.19 | async-start | bytes 1032192
  1557.3 243.1 %reduce-scatter.25.cloned.1.call-start = ((), (), s32[]{:S(2)}) async-start(), calls=%async_computation.16 | async-start | bytes 442368
  1558.0 279.2 %reduce-scatter.27.cloned.1.call-start = ((), (), s32[]{:S(2)}) async-start(), calls=%async_computation.17 | async-start | bytes 442368
  1590.5 97.2 %copy-start.13 = (f32[1024,768]{0,1:T(8,128)S(1)}, f32[1024,768]{0,1:T(8,128)}, u32[]{:S(2)}) copy-start(f32[1024,768]{0,1:T(8,128)} %copy-done.11) | copy-start | bytes 9437188
  1590.5 97.3 %copy-start.94 = (f32[1024]{0:T(1024)S(1)}, f32[1024]{0:T(1024)}, u32[]{:S(2)}) copy-start(f32[1024]{0:T(1024)} %copy-done.92) | copy-start | bytes 12292
  1594.3 325.7 %all-reduce.54.cloned.1.call-start = ((), (), s32[]{:S(2)}) async-start(), calls=%async_computation.20 | async-start | bytes 3735552 | tf_op jit(solution)/shard_map/psum | solution.py:217
  (118 other events, 850.4 us)
Sparse Core Ops, SparseCore 0:
  10.5 43.5 all-gather.18
  55.9 28.9 all-gather.20
  86.9 40.5 all-gather.22
  129.2 29.0 all-gather.24
  1062.3 54.2 reduce-scatter.20
  1454.3 54.0 reduce-scatter.22
  1519.9 81.4 reduce-scatter.16
  1605.4 80.1 reduce-scatter.18
  1688.8 35.5 reduce-scatter.28
  1728.0 35.4 reduce-scatter.30
  1766.5 33.8 reduce-scatter.24
  1803.3 33.8 reduce-scatter.26
  1839.8 80.1 all-reduce.53
where the time goes:
time: 1950 us; the launch traced here: 1930 us
  local copies, waits for them, and re-layouts  582 us (30%)
  matrix products  579 us (30%)
  other arithmetic  354 us (18%)
  waiting for transfers between devices  243 us (12%)
  blocking collectives  150 us (8%)
  between operations  19.7 us (1%)
    dot_general x24, matrix products, block_step(): inside = jnp.einsum('hij,jhp->ihp', mixing, values_block, precision=HIGHEST)  234 us
    unnamed x17, waiting for transfers between devices  98.5 us
    dot_general x24, matrix products, block_step(): jnp.einsum('jh,jhp,jn->hpn', weight_last, values_block, b_block, precisio...  88.8 us
    dot_general x32, matrix products, block_step(): outside = jnp.einsum('in,hpn->ihp', c_block, carry_state, precision=HIGHEST)  85.4 us
    reduce_scatter x2, waiting for transfers between devices, shards(): lax.psum_scatter(matrices[0], 'fsdp', scatter_dimension=0, tiled=True)  85.1 us
    unnamed x265, local copies, waits for them, and re-layouts  80.1 us
    slice x2, local copies, waits for them, and re-layouts, mixer(): summed = conv_bias[None, :] + conv_weight[kernel - 1][None, :] * conv_in  76.3 us
    another operation x94, local copies, waits for them, and re-layouts  63.2 us
  transfers between devices with their start and end apart: 13, of which 6 were waited for; matrix products, arithmetic and copies ran while one was open for 51% of the time, Pallas kernels for 0%

commit v1 on v0

v1 whole, which is shorter than its diff:
```python
import functools

import jax
import jax.numpy as jnp
from jax import lax
from jax.experimental import pallas as pl
from jax.experimental.pallas import tpu as pltpu
from jax.sharding import PartitionSpec as P

EPSILON = 1e-05
ROWS = 256
CHUNK = 128
LANES = 128
HALO = 8
HIGHEST = lax.Precision.HIGHEST
F32 = jnp.float32
BF16 = jnp.bfloat16
VMEM_BYTES = 56 * 1024 * 1024


def dot_nn(left, right, precision=None):
    return lax.dot_general(
        left, right, (((1,), (0,)), ((), ())), preferred_element_type=F32, precision=precision
    )


def dot_nt(left, right):
    return lax.dot_general(left, right, (((1,), (1,)), ((), ())), preferred_element_type=F32)


def dot_tn(left, right):
    return lax.dot_general(left, right, (((0,), (0,)), ((), ())), preferred_element_type=F32)


def sigmoid(v):
    return 0.5 * jnp.tanh(0.5 * v) + 0.5


def softplus(v):
    return jnp.maximum(v, 0.0) + jnp.log1p(jnp.exp(-jnp.abs(v)))


def iota2(shape, axis):
    return lax.broadcasted_iota(jnp.int32, shape, axis)


def column(values, index):
    return values[:, index : index + 1]


def spread(values, pair, low_half):
    return jnp.where(low_half, column(values, 2 * pair), column(values, 2 * pair + 1))


def convolve(ext_ref, taps_ref, bias_ref, masks, at):
    rows = masks.shape[0]
    cols = pl.ds(at, LANES)
    total = bias_ref[:, cols] + taps_ref[3:4, cols] * ext_ref[HALO : HALO + rows, cols]
    for back in range(1, 4):
        shifted = ext_ref[HALO - back : HALO - back + rows, cols]
        total = total + taps_ref[3 - back : 4 - back, cols] * shifted * column(masks, back - 1)
    return total


def forward_kernel(
    sizes,
    h_ref, masks_ref, segr_ref, w_ref, wout_ref, taps_ref, cbias_ref, gin_ref, ggate_ref,
    head_ref, skip_ref,
    next_ref, normed_ref, proj_ref, y_ref, gated_ref, states_ref,
    ext, xs, state,
):
    inner, xbc, nstate, pairs = sizes
    rows = h_ref.shape[0]

    @pl.when(pl.program_id(0) == 0)
    def _():
        state[...] = jnp.zeros_like(state)
        ext[0:HALO, :] = jnp.zeros((HALO, xbc), F32)

    hidden = h_ref[...].astype(F32)
    scale = lax.rsqrt(jnp.mean(hidden * hidden, axis=-1, keepdims=True) + EPSILON)
    normed_ref[...] = (hidden * scale * gin_ref[...]).astype(BF16)
    proj_ref[...] = dot_nn(normed_ref[...], w_ref[...])
    masks = masks_ref[...]
    ext[HALO : HALO + rows, :] = proj_ref[:, inner : inner + xbc]
    for at in range(0, xbc, LANES):
        v = convolve(ext, taps_ref, cbias_ref, masks, at)
        xs[:, at : at + LANES] = v * sigmoid(v)
    ext[0:HALO, :] = ext[rows : rows + HALO, :]

    low_half = iota2((CHUNK, LANES), 1) < LANES // 2
    low_row = iota2((1, LANES), 1) < LANES // 2
    t_at, s_at = iota2((CHUNK, CHUNK), 0), iota2((CHUNK, CHUNK), 1)
    tri = (t_at >= s_at).astype(F32)

    @pl.loop(0, rows // CHUNK)
    def _(c):
        span = pl.ds(pl.multiple_of(c * CHUNK, CHUNK), CHUNK)
        mk = masks_ref[span, :]
        dt = softplus(proj_ref[span, inner + xbc : inner + xbc + LANES] + head_ref[0:1, :])
        cum = dot_nn(tri, -head_ref[1:2, :] * dt, HIGHEST)
        cum_t, dt_t = cum.T, dt.T
        segr = segr_ref[c]
        bias = jnp.where((t_at >= s_at) & (column(mk, 8) == segr), 0.0, -1e30)
        b_f = xs[span, inner : inner + nstate]
        c_b = xs[span, inner + nstate : inner + 2 * nstate].astype(BF16)
        both = dot_nt(c_b, b_f.astype(BF16))
        b_t = b_f.T.astype(BF16)
        last = cum[CHUNK - 1 : CHUNK, :]
        from_state = jnp.exp(cum) * column(mk, 3)
        to_state = jnp.exp(last - cum) * column(mk, 4) * dt
        keep = jnp.exp(last) * mk[CHUNK - 1 : CHUNK, 3:4]
        for pair in range(pairs):
            cols = pl.ds(pair * LANES, LANES)
            x = xs[span, cols]
            x_b = x.astype(BF16)
            parts = []
            for head in (2 * pair, 2 * pair + 1):
                decay = jnp.exp(column(cum, head) - cum_t[head : head + 1, :] + bias)
                mix = decay * both * dt_t[head : head + 1, :]
                parts.append(dot_nn(mix.astype(BF16), x_b))
            inside = jnp.where(low_half, parts[0], parts[1])
            old = state[:, cols]
            states_ref[c, :, cols] = old
            outside = dot_nn(c_b, old.astype(BF16)) * spread(from_state, pair, low_half)
            fresh = dot_nn(b_t, (x * spread(to_state, pair, low_half)).astype(BF16))
            state[:, cols] = old * spread(keep, pair, low_row) + fresh
            y_ref[span, cols] = inside + outside + skip_ref[:, cols] * x

    total = jnp.zeros((rows, LANES), F32)
    for at in range(0, inner, LANES):
        z = proj_ref[:, at : at + LANES]
        g = y_ref[:, at : at + LANES] * (z * sigmoid(z))
        xs[:, at : at + LANES] = g
        total = total + g * g
    scale = lax.rsqrt(jnp.sum(total, axis=-1, keepdims=True) / inner + EPSILON)
    for at in range(0, inner, LANES):
        g = xs[:, at : at + LANES] * scale * ggate_ref[:, at : at + LANES]
        gated_ref[:, at : at + LANES] = g.astype(BF16)
    out = h_ref[...].astype(F32) + dot_nn(gated_ref[...], wout_ref[...])
    next_ref[...] = out.astype(next_ref.dtype)


def backward_kernel(
    sizes,
    dh_ref, h_ref, masks_ref, segr_ref, proj_ref, before_ref, y_ref, states_ref,
    w_ref, wout_ref, taps_ref, cbias_ref, gin_ref, ggate_ref, head_ref, skip_ref, fold_ref,
    dnext_ref, dproj_ref, sg_gate, sg_conv, sg_in, sg_skip, sg_head,
    ext, xs, conv, dy, dxs, dstate, rowsc, flat,
):
    inner, xbc, nstate, pairs = sizes
    rows = h_ref.shape[0]
    step = pl.program_id(0)

    @pl.when(step == 0)
    def _():
        dstate[...] = jnp.zeros_like(dstate)
        rowsc[...] = jnp.zeros_like(rowsc)
        flat[...] = jnp.zeros_like(flat)
        dxs[rows : rows + HALO, :] = jnp.zeros((HALO, xbc), F32)
        for ref in (sg_gate, sg_conv, sg_in, sg_skip, sg_head):
            ref[...] = jnp.zeros_like(ref)

    dh = dh_ref[...].astype(F32)
    dy[...] = dot_nt(dh.astype(BF16), wout_ref[...])

    squares = jnp.zeros((rows, LANES), F32)
    cross = jnp.zeros((rows, LANES), F32)
    for at in range(0, inner, LANES):
        cols = pl.ds(at, LANES)
        z = proj_ref[:, cols]
        g = y_ref[:, cols] * (z * sigmoid(z))
        squares = squares + g * g
        cross = cross + g * (dy[:, cols] * ggate_ref[:, cols])
    scale = lax.rsqrt(jnp.sum(squares, axis=-1, keepdims=True) / inner + EPSILON)
    mean = scale * jnp.sum(cross, axis=-1, keepdims=True) / inner
    for at in range(0, inner, LANES):
        cols = pl.ds(at, LANES)
        z = proj_ref[:, cols]
        sig = sigmoid(z)
        gate = z * sig
        y = y_ref[:, cols]
        m = y * gate * scale
        dgated = dy[:, cols]
        sg_gate[0:1, cols] += jnp.sum(m * dgated, axis=0, keepdims=True)
        dg = scale * (dgated * ggate_ref[:, cols] - m * mean)
        dproj_ref[:, cols] = (dg * y * (sig * (1.0 + z * (1.0 - sig)))).astype(BF16)
        dy[:, cols] = dg * gate

    masks = masks_ref[...]
    ext[0:HALO, :] = before_ref[:, inner : inner + xbc]
    ext[HALO : HALO + rows, :] = proj_ref[:, inner : inner + xbc]
    for at in range(0, xbc, LANES):
        v = convolve(ext, taps_ref, cbias_ref, masks, at)
        conv[:, at : at + LANES] = v
        xs[:, at : at + LANES] = v * sigmoid(v)

    low_half = iota2((CHUNK, LANES), 1) < LANES // 2
    low_row = iota2((1, LANES), 1) < LANES // 2
    lane = iota2((CHUNK, LANES), 1)
    s_at, t_at = iota2((CHUNK, CHUNK), 0), iota2((CHUNK, CHUNK), 1)
    tri = (s_at >= t_at).astype(F32)
    tri_t = (s_at <= t_at).astype(F32)
    last_row = iota2((CHUNK, LANES), 0) == CHUNK - 1
    chunks = rows // CHUNK

    @pl.loop(0, chunks)
    def _(back):
        c = chunks - 1 - back
        span = pl.ds(pl.multiple_of(c * CHUNK, CHUNK), CHUNK)
        mk = masks_ref[span, :]
        raw = proj_ref[span, inner + xbc : inner + xbc + LANES] + head_ref[0:1, :]
        dt = softplus(raw)
        speed = head_ref[1:2, :]
        cum = dot_nn(tri, -speed * dt, HIGHEST)
        cum_t = cum.T
        segr = segr_ref[c]
        bias = jnp.where((s_at <= t_at) & (column(mk, 8) == segr), 0.0, -1e30)
        b_b = xs[span, inner : inner + nstate].astype(BF16)
        c_f = xs[span, inner + nstate : inner + 2 * nstate]
        c_b = c_f.astype(BF16)
        c_t = c_f.T.astype(BF16)
        both = dot_nt(b_b, c_b)
        last = cum[CHUNK - 1 : CHUNK, :]
        from_state = jnp.exp(cum) * column(mk, 3)
        to_bare = jnp.exp(last - cum) * column(mk, 4)
        to_state = to_bare * dt
        keep = jnp.exp(last) * mk[CHUNK - 1 : CHUNK, 3:4]
        dboth = jnp.zeros((CHUNK, CHUNK), F32)
        db = jnp.zeros((CHUNK, nstate), F32)
        dc = jnp.zeros((CHUNK, nstate), F32)
        ddt = jnp.zeros((CHUNK, LANES), F32)
        dto = jnp.zeros((CHUNK, LANES), F32)
        dfrom = jnp.zeros((CHUNK, LANES), F32)
        for pair in range(pairs):
            cols = pl.ds(pair * LANES, LANES)
            x = xs[span, cols]
            d = dy[span, cols]
            d_b = d.astype(BF16)
            old = states_ref[c, :, cols]
            old_b = old.astype(BF16)
            dnew = dstate[:, cols]
            dnew_b = dnew.astype(BF16)
            weight = spread(to_state, pair, low_half)
            scaled = d * spread(from_state, pair, low_half)
            scaled_b = scaled.astype(BF16)
            reach = scaled * dot_nn(c_b, old_b)
            pull = dot_nn(b_b, dnew_b)
            dc = dc + dot_nt(scaled_b, old_b)
            db = db + dot_nt((x * weight).astype(BF16), dnew_b)
            flat[0:1, cols] = jnp.sum(dnew * old, axis=0, keepdims=True)
            dstate[:, cols] = dot_nn(c_t, scaled_b) + dnew * spread(keep, pair, low_row)
            gain = x * pull
            parts = []
            for head in (2 * pair, 2 * pair + 1):
                mine = low_half if head % 2 == 0 else jnp.logical_not(low_half)
                dt_col = column(dt, head)
                x_m = jnp.where(mine, x, 0.0).astype(BF16)
                decay = jnp.exp(cum_t[head : head + 1, :] - column(cum, head) + bias)
                prod = dot_nt(x_m, d_b)
                mix = decay * both
                parts.append(dot_nn(mix.astype(BF16), d_b))
                inner_prod = mix * prod
                dboth = dboth + decay * prod * dt_col
                rowsc[head : head + 1, :] = jnp.sum(inner_prod * dt_col, axis=0, keepdims=True)
                here = lane == head
                ddt = jnp.where(here, jnp.sum(inner_prod, axis=1, keepdims=True), ddt)
                dto = jnp.where(
                    here, jnp.sum(jnp.where(mine, gain, 0.0), axis=1, keepdims=True), dto
                )
                dfrom = jnp.where(
                    here, jnp.sum(jnp.where(mine, reach, 0.0), axis=1, keepdims=True), dfrom
                )
            inside = jnp.where(low_half, parts[0], parts[1]) * spread(dt, pair, low_half)
            dxs[span, cols] = inside + weight * pull + skip_ref[:, cols] * d
            sg_skip[0:1, cols] += jnp.sum(d * x, axis=0, keepdims=True)
        dxs[span, inner : inner + nstate] = db + dot_nn(dboth.astype(BF16), c_b)
        dxs[span, inner + nstate : inner + 2 * nstate] = dc + dot_nn(dboth.T.astype(BF16), b_b)
        moved = dto * to_state
        dlast = dot_nn(flat[...], fold_ref[...], HIGHEST)[0:1, :] * keep
        dlast = dlast + jnp.sum(moved, axis=0, keepdims=True)
        dcum = rowsc[...].T + dfrom - dt * ddt - moved
        dcum = dcum + jnp.where(last_row, dlast, 0.0)
        drate = dot_nn(tri_t, dcum, HIGHEST)
        dtotal = ddt + dto * to_bare - speed * drate
        draw = dtotal * sigmoid(raw)
        dproj_ref[span, inner + xbc : inner + xbc + LANES] = draw.astype(BF16)
        sg_head[0:1, :] += jnp.sum(draw, axis=0, keepdims=True)
        sg_head[1:2, :] += jnp.sum(-speed * dt * drate, axis=0, keepdims=True)

    for at in range(0, xbc, LANES):
        cols = pl.ds(at, LANES)
        v = conv[:, cols]
        sig = sigmoid(v)
        dconv = dxs[0:rows, cols] * (sig * (1.0 + v * (1.0 - sig)))
        dxs[0:rows, cols] = dconv
        sg_conv[4:5, cols] += jnp.sum(dconv, axis=0, keepdims=True)
        sg_conv[3:4, cols] += jnp.sum(dconv * ext[HALO : HALO + rows, cols], axis=0, keepdims=True)
        total = dconv * taps_ref[3:4, cols]
        for back in range(1, 4):
            shifted = ext[HALO - back : HALO - back + rows, cols] * column(masks, back - 1)
            sg_conv[3 - back : 4 - back, cols] += jnp.sum(dconv * shifted, axis=0, keepdims=True)
            later = dxs[back : back + rows, cols] * column(masks, 4 + back)
            total = total + later * taps_ref[3 - back : 4 - back, cols]
        dproj_ref[:, inner + at : inner + at + LANES] = total.astype(BF16)
    dxs[rows : rows + HALO, :] = dxs[0:HALO, :]

    dnormed = dot_nt(dproj_ref[...], w_ref[...])
    hidden = h_ref[...].astype(F32)
    scale = lax.rsqrt(jnp.mean(hidden * hidden, axis=-1, keepdims=True) + EPSILON)
    m = hidden * scale
    sg_in[0:1, :] += jnp.sum(m * dnormed, axis=0, keepdims=True)
    dm = dnormed * gin_ref[...]
    dnext_ref[...] = dh_ref[...].astype(F32) + scale * (
        dm - m * jnp.mean(dm * m, axis=-1, keepdims=True)
    )


def whole(array):
    return pl.BlockSpec(array.shape, lambda i: (0,) * array.ndim)


def dims(hidden, weights):
    length, width = hidden.shape
    inner = weights["w_out"].shape[0]
    xbc = weights["taps"].shape[1]
    nstate = (xbc - inner) // 2
    return length, width, inner, xbc, nstate, inner // LANES


def run_forward(hidden, masks, segr, weights, heads, skip, out_type):
    length, width, inner, xbc, nstate, pairs = dims(hidden, weights)
    packed = inner + xbc + LANES
    steps = length // ROWS
    per = ROWS // CHUNK

    def rows(cols):
        return pl.BlockSpec((ROWS, cols), lambda i: (i, 0))

    fixed = (weights["w"], weights["w_out"], weights["taps"], weights["cbias"], weights["g_in"],
             weights["g_gate"], heads, skip)
    return pl.pallas_call(
        functools.partial(forward_kernel, (inner, xbc, nstate, pairs)),
        grid=(steps,),
        in_specs=[rows(width), rows(masks.shape[1]),
                  pl.BlockSpec((per, 1, CHUNK), lambda i: (i, 0, 0))] + [whole(a) for a in fixed],
        out_specs=[rows(width), rows(width), rows(packed), rows(inner), rows(inner),
                   pl.BlockSpec((per, nstate, inner), lambda i: (i, 0, 0))],
        out_shape=[
            jax.ShapeDtypeStruct((length, width), out_type),
            jax.ShapeDtypeStruct((length, width), BF16),
            jax.ShapeDtypeStruct((length, packed), F32),
            jax.ShapeDtypeStruct((length, inner), F32),
            jax.ShapeDtypeStruct((length, inner), BF16),
            jax.ShapeDtypeStruct((length // CHUNK, nstate, inner), F32),
        ],
        scratch_shapes=[
            pltpu.VMEM((ROWS + HALO, xbc), F32),
            pltpu.VMEM((ROWS, xbc), F32),
            pltpu.VMEM((nstate, inner), F32),
        ],
        compiler_params=pltpu.CompilerParams(vmem_limit_bytes=VMEM_BYTES),
        cost_estimate=pl.CostEstimate(
            flops=60_000_000_000, bytes_accessed=60_000_000, transcendentals=6_000_000),
        name="layer_forward",
    )(hidden, masks, segr, *fixed)


def run_backward(grad, hidden, masks, segr, saved, weights, heads, skip, fold):
    length, width, inner, xbc, nstate, pairs = dims(hidden, weights)
    packed = inner + xbc + LANES
    steps = length // ROWS
    per = ROWS // CHUNK
    proj, y, states = saved

    def rows(cols):
        return pl.BlockSpec((ROWS, cols), lambda i: (steps - 1 - i, 0))

    def before(i):
        return (jnp.maximum((steps - 1 - i) * (ROWS // HALO) - 1, 0), 0)

    fixed = (weights["w"], weights["w_out"], weights["taps"], weights["cbias"], weights["g_in"],
             weights["g_gate"], heads, skip, fold)
    sums = [(8, inner), (8, xbc), (8, width), (8, inner), (8, LANES)]
    return pl.pallas_call(
        functools.partial(backward_kernel, (inner, xbc, nstate, pairs)),
        grid=(steps,),
        in_specs=[rows(width), rows(width), rows(masks.shape[1]),
                  pl.BlockSpec((per, 1, CHUNK), lambda i: (steps - 1 - i, 0, 0)),
                  rows(packed), pl.BlockSpec((HALO, packed), before), rows(inner),
                  pl.BlockSpec((per, nstate, inner), lambda i: (steps - 1 - i, 0, 0))]
        + [pl.BlockSpec(a.shape, lambda i: (0, 0), pipeline_mode=pl.Buffered(1)) for a in fixed],
        out_specs=[rows(width), rows(packed)] + [pl.BlockSpec(s, lambda i: (0, 0)) for s in sums],
        out_shape=[
            jax.ShapeDtypeStruct((length, width), F32),
            jax.ShapeDtypeStruct((length, packed), BF16),
        ] + [jax.ShapeDtypeStruct(s, F32) for s in sums],
        scratch_shapes=[
            pltpu.VMEM((ROWS + HALO, xbc), F32),
            pltpu.VMEM((ROWS, xbc), F32),
            pltpu.VMEM((ROWS, xbc), F32),
            pltpu.VMEM((ROWS, inner), F32),
            pltpu.VMEM((ROWS + HALO, xbc), F32),
            pltpu.VMEM((nstate, inner), F32),
            pltpu.VMEM((LANES, CHUNK), F32),
            pltpu.VMEM((8, inner), F32),
        ],
        compiler_params=pltpu.CompilerParams(vmem_limit_bytes=VMEM_BYTES),
        cost_estimate=pl.CostEstimate(
            flops=120_000_000_000, bytes_accessed=80_000_000, transcendentals=6_000_000),
        name="layer_backward",
    )(grad, hidden, masks, segr, proj, proj, y, states, *fixed)


def token_masks(segment):
    length = segment.shape[0]
    blocks = segment.reshape(length // CHUNK, CHUNK)
    keeps, laters = [], []
    for back in range(1, 4):
        same = (segment[back:] == segment[:-back]).astype(F32)
        keeps.append(jnp.pad(same, (back, 0)))
        laters.append(jnp.pad(same, (0, back)))
    before = jnp.concatenate([jnp.full((1,), -1, jnp.int32), blocks[:-1, -1]])
    carried = (blocks == before[:, None]).astype(F32).reshape(length)
    lasting = (blocks == blocks[:, -1:]).astype(F32).reshape(length)
    number = segment.astype(F32)
    columns = keeps + [carried, lasting] + laters + [number]
    masks = jnp.pad(jnp.stack(columns, axis=1), ((0, 0), (0, 16 - len(columns))))
    return masks, number.reshape(length // CHUNK, 1, CHUNK)


def gather_layer(w_in, w_dt, w_out, conv_w, conv_b, norm_in, norm_gate, heads):
    wide = jnp.concatenate([w_in, jnp.pad(w_dt, ((0, 0), (0, LANES - heads)))], axis=1)
    small = jnp.concatenate([conv_w.reshape(-1), conv_b, norm_in, norm_gate])
    taps, chan, gain_in, gain_gate = conv_w.shape[0], conv_b.shape[0], norm_in.size, norm_gate.size
    wide = lax.all_gather(wide, "fsdp", axis=0, tiled=True)
    w_out = lax.all_gather(w_out, "fsdp", axis=0, tiled=True)
    small = lax.all_gather(small, "fsdp", axis=0).astype(F32)
    cut = taps * chan
    conv = small[:, :cut].reshape(-1, taps, chan).transpose(1, 0, 2).reshape(taps, -1)
    return {
        "w": wide,
        "w_out": w_out,
        "taps": jnp.pad(conv, ((0, 8 - taps), (0, 0))),
        "cbias": small[:, cut : cut + chan].reshape(1, -1),
        "g_in": small[:, cut + chan : cut + chan + gain_in].reshape(1, -1),
        "g_gate": small[:, cut + chan + gain_in :].reshape(1, -1),
    }


def owned_sum(values):
    part = lax.psum_scatter(values.astype(BF16), "fsdp", scatter_dimension=0, tiled=True)
    return lax.psum(part, "rep").astype(F32)


def shards(
    tokens, segments, w_in, w_dt, w_out, conv_w, conv_b, norm_in, norm_gate,
    dt_bias, a_log, d_skip, cotangent,
):
    layers, heads = dt_bias.shape
    group = lax.axis_size("fsdp")
    masks, segr = token_masks(segments[0])
    headdim = w_out.shape[1] * group // heads
    inner = heads * headdim
    fold = (jnp.arange(inner)[:, None] // headdim == jnp.arange(LANES)[None, :]).astype(F32)
    weights, head_rows, skips = [], [], []
    for l in range(layers):
        weights.append(gather_layer(
            w_in[l], w_dt[l], w_out[l], conv_w[l], conv_b[l], norm_in[l], norm_gate[l], heads))
        both = jnp.stack([dt_bias[l], jnp.exp(a_log[l])])
        head_rows.append(jnp.pad(both, ((0, 6), (0, LANES - heads))))
        skips.append(jnp.repeat(d_skip[l], headdim)[None, :])
    hiddens, saved = [tokens[0]], []
    for l in range(layers):
        out_type = BF16 if l == layers - 1 else F32
        following, normed, proj, y, gated, states = run_forward(
            hiddens[l], masks, segr, weights[l], head_rows[l], skips[l], out_type)
        hiddens.append(following)
        saved.append((normed, gated, (proj, y, states)))
    grad = cotangent[0]
    wide, outs, smalls, per_head = [None] * layers, [None] * layers, [None] * layers, [None] * layers
    for l in reversed(range(layers)):
        normed, gated, kept = saved[l]
        outs[l] = owned_sum(dot_tn(gated, grad.astype(BF16)))
        grad, dproj, s_gate, s_conv, s_in, s_skip, s_head = run_backward(
            grad, hiddens[l], masks, segr, kept, weights[l], head_rows[l], skips[l], fold)
        wide[l] = owned_sum(dot_tn(normed, dproj))
        smalls[l] = jnp.concatenate([
            s_conv[:5].reshape(5, group, -1).transpose(1, 0, 2).reshape(group, -1),
            s_in[0].reshape(group, -1),
            s_gate[0].reshape(group, -1),
        ], axis=1)
        per_head[l] = jnp.stack([
            s_head[0, :heads], s_head[1, :heads], s_skip[0].reshape(heads, headdim).sum(-1)])
    small = jnp.stack(smalls, axis=1)
    small = lax.psum_scatter(small, "fsdp", scatter_dimension=0, tiled=True)[0]
    small = lax.psum(small, "rep")
    chan, gain = conv_b.shape[1], norm_in.shape[1]
    columns = w_in.shape[2]
    head_sums = lax.psum(jnp.stack(per_head, axis=1), ("rep", "fsdp"))
    wide = jnp.stack(wide)
    return (
        hiddens[-1][None],
        grad[None],
        wide[:, :, :columns],
        wide[:, :, columns : columns + heads],
        jnp.stack(outs),
        small[:, : 4 * chan].reshape(layers, 4, chan),
        small[:, 4 * chan : 5 * chan],
        small[:, 5 * chan : 5 * chan + gain],
        small[:, 5 * chan + gain :],
        head_sums[0],
        head_sums[1],
        head_sums[2],
    )


def solution(mesh):
    sharded = P(None, "fsdp", None)
    tokens = P(("rep", "fsdp"), None, None)
    narrow = P(None, "fsdp")
    return jax.shard_map(
        shards,
        mesh=mesh,
        in_specs=(
            tokens, P(("rep", "fsdp"), None), sharded, sharded, sharded, P(None, None, "fsdp"),
            narrow, narrow, narrow, P(), P(), P(), tokens,
        ),
        out_specs=(
            tokens, tokens, sharded, sharded, sharded, P(None, None, "fsdp"),
            narrow, narrow, narrow, P(), P(), P(),
        ),
        check_vma=False,
    )
```

time: 1950 us -> 693 us (0.36)
  local copies, waits for them, and re-layouts: 582 us -> 31.2 us
  matrix products: 579 us -> 33.4 us
  other arithmetic: 354 us -> 8.64 us
  Pallas kernels: 0 us -> 274 us
  blocking collectives: 150 us -> 78.3 us
    dot_general x128 -> x4, matrix products: 577 us -> 33.4 us  [dot_tn(): lax.dot_general(left, right, (((0,), (0,)), ((), ())), preferred_element_...]
    pallas_call x0 -> x4, Pallas kernels: none -> 274 us  [the longest x2 195 us: run_backward(): pl.pallas_call(functools.partial(backward_kernel, (inner, xbc, nstate, pa...]
    reshape x26 -> x19, local copies, waits for them, and re-layouts: 129 us -> 5.46 us  [the longest x2 1.35 us: gather_layer(): small[:, cut:cut + chan].reshape(1, -1)]
    slice x55 -> x29, local copies, waits for them, and re-layouts: 119 us -> 13.3 us  [the longest x1 1.9 us: shards(): w_out[l]]
    reduce_sum x26 -> x2, other arithmetic: 103 us -> 0.23 us  [shards(): s_skip[0].reshape(heads, headdim).sum(-1)]
    unnamed x17 -> x11, waiting for transfers between devices: 98.5 us -> 11.2 us
    unnamed x265 -> x44, local copies, waits for them, and re-layouts: 80.1 us -> 3.84 us
    all_gather x4, waiting for transfers between devices: 0.06 us -> 74.4 us  [the longest x2 74.4 us: gather_layer(): wide = lax.all_gather(wide, 'fsdp', axis=0, tiled=True)]
  transfers between devices with their start and end apart: 13 -> 10, of which waited for: 6 -> 6; matrix products, arithmetic and copies ran while one was open for 51% -> 8% of each run, Pallas kernels for 0% -> 20%
where the time goes in v1:
time: 693 us; the launch traced here: 689 us
  Pallas kernels  274 us (40%)
  waiting for transfers between devices  248 us (36%)
  blocking collectives  78.3 us (11%)
  matrix products  33.4 us (5%)
  local copies, waits for them, and re-layouts  31.2 us (5%)
  between operations  14.8 us (2%)
  other arithmetic  8.64 us (1%)
    pallas_call x2, Pallas kernels, run_backward(): pl.pallas_call(functools.partial(backward_kernel, (inner, xbc, nstate, pa...  195 us
    reduce_scatter x4, waiting for transfers between devices, owned_sum(): lax.psum_scatter(values.astype(BF16), 'fsdp', scatter_dimension=0, tiled=...  100 us
    pallas_call x2, Pallas kernels, run_forward(): pl.pallas_call(functools.partial(forward_kernel, (inner, xbc, nstate, pai...  78.6 us
    all_gather x2, waiting for transfers between devices, gather_layer(): wide = lax.all_gather(wide, 'fsdp', axis=0, tiled=True)  74.4 us
    psum x1, waiting for transfers between devices, owned_sum(): return lax.psum(part, 'rep').astype(F32)  62.5 us
    psum x1, blocking collectives, shards(): head_sums = lax.psum(jnp.stack(per_head, axis=1), ('rep', 'fsdp'))  39.4 us
    dot_general x4, matrix products, dot_tn(): lax.dot_general(left, right, (((0,), (0,)), ((), ())), preferred_element_...  33.4 us
    all_gather x2, blocking collectives, gather_layer(): small = lax.all_gather(small, 'fsdp', axis=0).astype(F32)  19.7 us
  transfers between devices with their start and end apart: 10, of which 6 were waited for; matrix products, arithmetic and copies ran while one was open for 8% of the time, Pallas kernels for 20%

profile of v1, /device:TPU:0, one launch (start us, length us, event | category | flops | bytes accessed | tf_op | source)
XLA Modules:
  0.0 688.6 jit_solution(17489647424908788137)
XLA Ops:
  7.2 1.9 fusion.10
  10.0 1.4 slice_bitcast_fusion
  11.5 0.9 fusion.4
  13.3 0.9 fusion.5
  14.7 10.6 %all-gather.4 = bf16[8,1,1408]{2,1,0:T(2,128)(2,1)S(1)} all-gather(bf16[1,1,1408]{2,1,0:T(2,128)(2,1)S(1)} %reshape.212), channel_id=3, replica_groups=mesh['rep'=4,'fsdp'=8] {'fsdp'}, dimensions={0}, use_global_device_ids=true | all-gather | bytes 25344 | tf_op jit(solution)/shard_map/all_gather | solution.py:438
  25.6 9.1 %all-gather.5 = bf16[8,1,1408]{2,1,0:T(2,128)(2,1)S(1)} all-gather(bf16[1,1,1408]{2,1,0:T(2,128)(2,1)S(1)} %reshape.214), channel_id=5, replica_groups=mesh['rep'=4,'fsdp'=8] {'fsdp'}, dimensions={0}, use_global_device_ids=true | all-gather | bytes 25344 | tf_op jit(solution)/shard_map/all_gather | solution.py:438
  36.8 0.8 pad.55.masks_ref
  45.9 1.2 fusion.3.fold_ref
  47.0 39.1 %all-gather.11.cloned.1.call-done.w_ref = bf16[768,3456]{1,0:T(8,128)(2,1)} async-done(((bf16[96,3456]{1,0:T(8,128)(2,1)}), bf16[768,3456]{1,0:T(8,128)(2,1)}) %all-gather.11.cloned.1.call-update) | async-done | bytes 5308432 | tf_op jit(solution)/shard_map/all_gather | solution.py:436
  86.1 39.4 %layer_forward.2 = (f32[1024,768]{1,0:T(8,128)}, bf16[1024,768]{1,0:T(8,128)(2,1)}, f32[1024,3456]{1,0:T(8,128)}, f32[1024,1536]{1,0:T(8,128)}, bf16[1024,1536]{1,0:T(8,128)(2,1)}, /*index=5*/f32[8,128,1536]{2,1,0:T(8,128)}) custom-call(bf16[1024,768]{1,0:T(8,128)(2,1)} %bitcast.133, f32[1024,16]{1,0:T(8,128)} %pad.55.masks_ref, ...), custom_call_target="tpu_custom_call" | custom-call | flops 60000002048 | bytes 60000000 | tf_op jit(solution)/shard_map/layer_forward/pallas_call | solution.py:342
  125.5 35.3 %all-gather.13.cloned.1.call-done.w_ref = bf16[768,3456]{1,0:T(8,128)(2,1)} async-done(((bf16[96,3456]{1,0:T(8,128)(2,1)}), bf16[768,3456]{1,0:T(8,128)(2,1)}) %all-gather.13.cloned.1.call-update) | async-done | bytes 5308432 | tf_op jit(solution)/shard_map/all_gather | solution.py:436
  160.8 39.2 %layer_forward.3 = (bf16[1024,768]{1,0:T(8,128)(2,1)}, bf16[1024,768]{1,0:T(8,128)(2,1)}, f32[1024,3456]{1,0:T(8,128)}, f32[1024,1536]{1,0:T(8,128)}, bf16[1024,...) custom-call(f32[1024,768]{1,0:T(8,128)} %get-tuple-element.38.h_ref, f32[1024,16]{1,0:T(8,128)} %pad.55.masks_ref, ...), custom_call_target="tpu_custom_call" | custom-call | flops 60000002048 | bytes 60000000 | tf_op jit(solution)/shard_map/layer_forward/pallas_call | solution.py:342
  200.0 97.6 %layer_backward.2 = (f32[1024,768]{1,0:T(8,128)}, bf16[1024,3456]{1,0:T(8,128)(2,1)}, f32[8,1536]{1,0:T(8,128)}, f32[8,1792]{1,0:T(8,128)}, f32[8,768]{1,0:T(8,1...) custom-call(bf16[1024,768]{1,0:T(8,128)(2,1)} %bitcast.132, f32[1024,768]{1,0:T(8,128)} %get-tuple-element.38.h_ref, ...), custom_call_target="tpu_custom_call" | custom-call | flops 120000004096 | bytes 80000000 | tf_op jit(solution)/shard_map/layer_backward/pallas_call | solution.py:385
  297.6 6.1 convolution_convert_fusion.3
  303.8 6.0 convolution_convert_fusion.2
  309.8 97.6 %layer_backward.3 = (f32[1024,768]{1,0:T(8,128)}, bf16[1024,3456]{1,0:T(8,128)(2,1)}, f32[8,1536]{1,0:T(8,128)}, f32[8,1792]{1,0:T(8,128)}, f32[8,768]{1,0:T(8,1...) custom-call(f32[1024,768]{1,0:T(8,128)} %get-tuple-element.43.dh_ref, bf16[1024,768]{1,0:T(8,128)(2,1)} %bitcast.134, ...), custom_call_target="tpu_custom_call" | custom-call | flops 120000004096 | bytes 80000000 | tf_op jit(solution)/shard_map/layer_backward/pallas_call | solution.py:385
  407.4 10.7 %convolution_convert_fusion.1 = bf16[768,3456]{1,0:T(8,128)(2,1)} fusion(bf16[1024,768]{1,0:T(8,128)(2,1)S(1)} %copy-done.15, bf16[1024,3456]{1,0:T(8,128)(2,1)} %get-tuple-element.49), kind=kOutput, calls=%fused_computation.1 | convolution fusion | flops 5438472192 | bytes 13959168 | tf_op jit(solution)/shard_map/dot_general | solution.py:32
  418.2 1.3 copy-done.16
  419.5 10.6 %convolution_convert_fusion = bf16[768,3456]{1,0:T(8,128)(2,1)} fusion(bf16[1024,768]{1,0:T(8,128)(2,1)S(1)} %copy-done.16, bf16[1024,3456]{1,0:T(8,128)(2,1)} %get-tuple-element.51), kind=kOutput, calls=%fused_computation | convolution fusion | flops 5438472192 | bytes 13959168 | tf_op jit(solution)/shard_map/dot_general | solution.py:32
  431.2 0.8 slice_reduce_fusion.3
  433.1 0.8 slice_reduce_fusion.2
  435.8 39.4 %reduce-scatter.5.cloned.1.call-done = bf16[96,3456]{1,0:T(8,128)(2,1)} async-done(((bf16[768,3456]{1,0:T(8,128)(2,1)}), bf16[96,3456]{1,0:T(8,128)(2,1)}) %reduce-scatter.5.cloned.1.call-update) | async-done | bytes 663568 | tf_op jit(solution)/shard_map/reduce_scatter | solution.py:452
  475.2 60.7 %reduce-scatter.7.cloned.1.call-done = bf16[96,3456]{1,0:T(8,128)(2,1)} async-done(((bf16[768,3456]{1,0:T(8,128)(2,1)}), bf16[96,3456]{1,0:T(8,128)(2,1)}) %reduce-scatter.7.cloned.1.call-update) | async-done | bytes 663568 | tf_op jit(solution)/shard_map/reduce_scatter | solution.py:452
  536.6 0.8 slice_reduce_fusion.1
  540.0 39.4 %psum.47 = f32[3,2,24]{2,0,1:T(4,128)S(1)} all-reduce(f32[3,2,24]{2,0,1:T(4,128)S(1)} %pad_maximum_fusion.1), channel_id=1, replica_groups=mesh['rep'=4,'fsdp'=8] {'rep','fsdp'}, use_global_device_ids=true, to_apply=%region_12.13 | all-reduce | flops 144 | bytes 1152 | tf_op jit(solution)/shard_map/psum | solution.py:500
  580.0 10.4 %all-reduce.18.cloned.1.call-done = f32[8,2,1408]{2,1,0:T(2,128)} async-done(((f32[8,2,1408]{2,1,0:T(2,128)}), f32[8,2,1408]{2,1,0:T(2,128)}) %all-reduce.18.cloned.1.call-update) | async-done | bytes 90128
  590.4 1.4 dynamic-slice_bitcast_fusion
  591.7 19.1 %psum.46 = f32[2,1408]{1,0:T(2,128)S(1)} all-reduce(f32[2,1408]{1,0:T(2,128)S(1)} %dynamic-slice_bitcast_fusion), channel_id=1, replica_groups=mesh['rep'=4,'fsdp'=8] {'rep'}, use_global_device_ids=true, to_apply=%region_9.10 | all-reduce | flops 2816 | bytes 22528 | tf_op jit(solution)/shard_map/psum | solution.py:497
  613.4 62.5 %all-reduce.20.cloned.1.call-done = (bf16[1,96,3456]{2,1,0:T(8,128)(2,1)}, bf16[1,96,3456]{2,1,0:T(8,128)(2,1)}, bf16[1,192,768]{2,1,0:T(8,128)(2,1)}, bf16[1,192,768]{2,1,0:T(8,128)(2,1)}) async-done(((bf16[1,96,3456]{2,1,0:T(8,128)(2,1)}, bf16[1,96,3456]{2,1,0:T(8,128)(2,1)}, bf16[1,192,768]{2,1,0:T(8,128)(2,1)}, bf16[1,192,768]{2,1,0:T(8,128)(2,1)}), (bf16[1,96,3456]{2,1,0:T(8,128)(2,1)}, ...) | async-done | bytes 1916944 | tf_op jit(solution)/shard_map/psum | solution.py:453
  676.7 1.5 maximum_convert_fusion
  678.8 1.6 slice.238
  680.5 1.1 maximum_convert_fusion.1
  (154 shorter events, 24.7 us)
Async XLA Ops:
  7.2 39.8 %all-gather.15.cloned.1.call-start = ((), (), s32[]{:S(2)}) async-start(), calls=%async_computation.10 | async-start | bytes 2654208 | tf_op jit(solution)/shard_map/all_gather | solution.py:437
  9.1 77.0 %all-gather.11.cloned.1.call-start = ((), (), s32[]{:S(2)}) async-start(), calls=%async_computation.4 | async-start | bytes 5971968 | tf_op jit(solution)/shard_map/all_gather | solution.py:436
  11.4 2.8 copy-start
  11.4 3.0 copy-start.7
  11.4 3.1 copy-start.5
  11.4 3.1 copy-start.6
  11.4 3.1 copy-start.8
  12.4 113.2 %all-gather.17.cloned.1.call-start = ((), (), s32[]{:S(2)}) async-start(), calls=%async_computation.11 | async-start | bytes 2654208 | tf_op jit(solution)/shard_map/all_gather | solution.py:437
  12.4 27.9 %copy-start.9 = (f32[2,24]{1,0:T(2,128)S(1)}, f32[2,24]{1,0:T(2,128)}, u32[]{:S(2)}) copy-start(f32[2,24]{1,0:T(2,128)} %param.24) | copy-start | bytes 580
  13.1 147.7 %all-gather.13.cloned.1.call-start = ((), (), s32[]{:S(2)}) async-start(), calls=%async_computation.5 | async-start | bytes 5971968 | tf_op jit(solution)/shard_map/all_gather | solution.py:436
  13.3 31.4 %copy-start.10 = (f32[2,24]{1,0:T(2,128)S(1)}, f32[2,24]{1,0:T(2,128)}, u32[]{:S(2)}) copy-start(f32[2,24]{1,0:T(2,128)} %param.23) | copy-start | bytes 580
  13.3 31.4 %copy-start.11 = (f32[2,24]{1,0:T(2,128)S(1)}, f32[2,24]{1,0:T(2,128)}, u32[]{:S(2)}) copy-start(f32[2,24]{1,0:T(2,128)} %param.22) | copy-start | bytes 580
  14.2 421.6 %reduce-scatter.9.cloned.1.call-start = ((), (), s32[]{:S(2)}) async-start(), calls=%async_computation.8 | async-start | bytes 2654208 | tf_op jit(solution)/shard_map/reduce_scatter | solution.py:452
  200.0 97.6 %copy-start.14 = (bf16[1024,1536]{1,0:T(8,128)(2,1)S(1)}, bf16[1024,1536]{1,0:T(8,128)(2,1)}, u32[]{:S(2)}) copy-start(bf16[1024,1536]{1,0:T(8,128)(2,1)} %get-tuple-element.52) | copy-start | bytes 9437188
  297.6 6.2 copy-start.12
  303.7 132.1 %reduce-scatter.11.cloned.1.call-start = ((), (), s32[]{:S(2)}) async-start(), calls=%async_computation.9 | async-start | bytes 2654208 | tf_op jit(solution)/shard_map/reduce_scatter | solution.py:452
  309.7 165.5 %reduce-scatter.5.cloned.1.call-start = ((), (), s32[]{:S(2)}) async-start(), calls=%async_computation.6 | async-start | bytes 5971968 | tf_op jit(solution)/shard_map/reduce_scatter | solution.py:452
  309.8 97.6 %copy-start.15 = (bf16[1024,768]{1,0:T(8,128)(2,1)S(1)}, bf16[1024,768]{1,0:T(8,128)(2,1)}, u32[]{:S(2)}) copy-start(bf16[1024,768]{1,0:T(8,128)(2,1)} %get-tuple-element.48) | copy-start | bytes 4718596
  418.1 1.4 copy-start.16
  418.1 117.8 %reduce-scatter.7.cloned.1.call-start = ((), (), s32[]{:S(2)}) async-start(), calls=%async_computation.7 | async-start | bytes 5971968 | tf_op jit(solution)/shard_map/reduce_scatter | solution.py:452
  430.2 0.8 copy-start.4
  430.2 2.8 copy-start.3
  430.2 105.8 %copy-start.13 = (u32[32]{0:T(128)S(1)}, u32[32]{0:T(128)}, u32[]{:S(2)}) copy-start(u32[32]{0:T(128)} %constant.57) | copy-start | bytes 388
  430.2 160.2 %all-reduce.18.cloned.1.call-start = ((), (), s32[]{:S(2)}) async-start(), calls=%async_computation.12 | async-start | bytes 180224
  435.7 240.2 %all-reduce.20.cloned.1.call-start = ((), (), s32[]{:S(2)}) async-start(), calls=%async_computation.13 | async-start | bytes 3833856 | tf_op jit(solution)/shard_map/psum | solution.py:453
  678.8 1.6 copy-start.1
  678.8 1.6 copy-start.2
Sparse Core Ops, SparseCore 0:
  10.5 31.7 all-gather.14
  44.7 41.3 all-gather.10
  88.0 29.0 all-gather.16
  119.4 41.3 all-gather.12
  303.8 42.4 reduce-scatter.8
  350.5 42.4 reduce-scatter.10
  418.3 56.9 reduce-scatter.4
  479.0 56.8 reduce-scatter.6
  539.6 50.7 all-reduce.17
  593.0 82.8 all-reduce.19

commit v2 on v1

--- a/solution.py
+++ b/solution.py
@@ -429,28 +429,44 @@
     return masks, number.reshape(length // CHUNK, 1, CHUNK)
 
 
-def gather_layer(w_in, w_dt, w_out, conv_w, conv_b, norm_in, norm_gate, heads):
-    wide = jnp.concatenate([w_in, jnp.pad(w_dt, ((0, 0), (0, LANES - heads)))], axis=1)
-    small = jnp.concatenate([conv_w.reshape(-1), conv_b, norm_in, norm_gate])
-    taps, chan, gain_in, gain_gate = conv_w.shape[0], conv_b.shape[0], norm_in.size, norm_gate.size
-    wide = lax.all_gather(wide, "fsdp", axis=0, tiled=True)
-    w_out = lax.all_gather(w_out, "fsdp", axis=0, tiled=True)
-    small = lax.all_gather(small, "fsdp", axis=0).astype(F32)
+def as_columns(flat, rows):
+    columns = -(-flat.shape[-1] // rows)
+    fill = rows * columns - flat.shape[-1]
+    flat = jnp.pad(flat, [(0, 0)] * (flat.ndim - 1) + [(0, fill)])
+    return flat.reshape(*flat.shape[:-1], rows, columns)
+
+
+def pack_layer(w_in, w_dt, conv_w, conv_b, norm_in, norm_gate):
+    rows = w_in.shape[0]
+    small = as_columns(jnp.concatenate([conv_w.reshape(-1), conv_b, norm_in, norm_gate]), rows)
+    unused = LANES - w_dt.shape[1] - small.shape[1]
+    return jnp.concatenate([w_in, w_dt, small, jnp.zeros((rows, unused), BF16)], axis=1)
+
+
+def unpack_layer(wide, w_out, start, rows, taps, chan, gain_in):
+    group = wide.shape[0] // rows
+    gain_gate = w_out.shape[0] // group
     cut = taps * chan
-    conv = small[:, :cut].reshape(-1, taps, chan).transpose(1, 0, 2).reshape(taps, -1)
+    count = cut + chan + gain_in + gain_gate
+    width = -(-count // rows)
+    small = wide[:, start : start + width].reshape(group, rows * width).astype(F32)
+    conv = small[:, :cut].reshape(group, taps, chan).transpose(1, 0, 2).reshape(taps, -1)
     return {
         "w": wide,
         "w_out": w_out,
         "taps": jnp.pad(conv, ((0, 8 - taps), (0, 0))),
         "cbias": small[:, cut : cut + chan].reshape(1, -1),
         "g_in": small[:, cut + chan : cut + chan + gain_in].reshape(1, -1),
-        "g_gate": small[:, cut + chan + gain_in :].reshape(1, -1),
+        "g_gate": small[:, cut + chan + gain_in : count].reshape(1, -1),
     }
 
 
-def owned_sum(values):
-    part = lax.psum_scatter(values.astype(BF16), "fsdp", scatter_dimension=0, tiled=True)
-    return lax.psum(part, "rep").astype(F32)
+def gather(array):
+    return lax.all_gather(array, "fsdp", axis=0, tiled=True)
+
+
+def scatter(array):
+    return lax.psum_scatter(array, "fsdp", scatter_dimension=0, tiled=True)
 
 
 def shards(
@@ -463,10 +479,15 @@
     headdim = w_out.shape[1] * group // heads
     inner = heads * headdim
     fold = (jnp.arange(inner)[:, None] // headdim == jnp.arange(LANES)[None, :]).astype(F32)
+    rows, columns = w_in.shape[1:]
+    taps, chan = conv_w.shape[1:]
+    gain = norm_in.shape[1]
+    used = columns + heads
     weights, head_rows, skips = [], [], []
     for l in range(layers):
-        weights.append(gather_layer(
-            w_in[l], w_dt[l], w_out[l], conv_w[l], conv_b[l], norm_in[l], norm_gate[l], heads))
+        packed = pack_layer(w_in[l], w_dt[l], conv_w[l], conv_b[l], norm_in[l], norm_gate[l])
+        weights.append(unpack_layer(
+            gather(packed), gather(w_out[l]), used, rows, taps, chan, gain))
         both = jnp.stack([dt_bias[l], jnp.exp(a_log[l])])
         head_rows.append(jnp.pad(both, ((0, 6), (0, LANES - heads))))
         skips.append(jnp.repeat(d_skip[l], headdim)[None, :])
@@ -478,40 +499,52 @@
         hiddens.append(following)
         saved.append((normed, gated, (proj, y, states)))
     grad = cotangent[0]
-    wide, outs, smalls, per_head = [None] * layers, [None] * layers, [None] * layers, [None] * layers
+    wides, outs = [None] * layers, [None] * layers
+    pending = []
     for l in reversed(range(layers)):
         normed, gated, kept = saved[l]
-        outs[l] = owned_sum(dot_tn(gated, grad.astype(BF16)))
+        out_grad = dot_tn(gated, grad.astype(BF16)).astype(BF16)
+        out_grad, grad = lax.optimization_barrier((out_grad, grad))
+        out_part = scatter(out_grad)
+        if pending:
+            part, grad = lax.optimization_barrier((pending[0], grad))
+            outs[l + 1] = lax.psum(part, "rep")
         grad, dproj, s_gate, s_conv, s_in, s_skip, s_head = run_backward(
             grad, hiddens[l], masks, segr, kept, weights[l], head_rows[l], skips[l], fold)
-        wide[l] = owned_sum(dot_tn(normed, dproj))
-        smalls[l] = jnp.concatenate([
+        per_head = jnp.concatenate([
+            s_head[0, :heads], s_head[1, :heads], s_skip[0].reshape(heads, headdim).sum(-1)])
+        small = jnp.concatenate([
             s_conv[:5].reshape(5, group, -1).transpose(1, 0, 2).reshape(group, -1),
             s_in[0].reshape(group, -1),
             s_gate[0].reshape(group, -1),
+            jnp.broadcast_to(per_head, (group, per_head.size)),
         ], axis=1)
-        per_head[l] = jnp.stack([
-            s_head[0, :heads], s_head[1, :heads], s_skip[0].reshape(heads, headdim).sum(-1)])
-    small = jnp.stack(smalls, axis=1)
-    small = lax.psum_scatter(small, "fsdp", scatter_dimension=0, tiled=True)[0]
-    small = lax.psum(small, "rep")
-    chan, gain = conv_b.shape[1], norm_in.shape[1]
-    columns = w_in.shape[2]
-    head_sums = lax.psum(jnp.stack(per_head, axis=1), ("rep", "fsdp"))
-    wide = jnp.stack(wide)
+        block = as_columns(small, rows)
+        block = block.reshape(group * rows, block.shape[-1]).astype(BF16)
+        wide = dot_tn(normed, dproj).astype(BF16)
+        wide = lax.dynamic_update_slice(wide, block, (0, used))
+        wides[l] = scatter(wide)
+        outs[l] = out_part
+        pending = [out_part]
+    *wides, outs[0] = lax.psum((*wides, outs[0]), "rep")
+    wide = jnp.stack(wides).astype(F32)
+    count = small.shape[1]
+    vectors = wide[:, :, used : used + block.shape[1]].reshape(layers, -1)[:, :count]
+    ends = [taps * chan, (taps + 1) * chan, (taps + 1) * chan + gain, count - 3 * heads]
+    per_head = vectors[:, ends[3] :].reshape(layers, 3, heads)
     return (
         hiddens[-1][None],
         grad[None],
         wide[:, :, :columns],
-        wide[:, :, columns : columns + heads],
-        jnp.stack(outs),
-        small[:, : 4 * chan].reshape(layers, 4, chan),
-        small[:, 4 * chan : 5 * chan],
-        small[:, 5 * chan : 5 * chan + gain],
-        small[:, 5 * chan + gain :],
-        head_sums[0],
-        head_sums[1],
-        head_sums[2],
+        wide[:, :, columns:used],
+        jnp.stack(outs).astype(F32),
+        vectors[:, : ends[0]].reshape(layers, taps, chan),
+        vectors[:, ends[0] : ends[1]],
+        vectors[:, ends[1] : ends[2]],
+        vectors[:, ends[2] : ends[3]],
+        per_head[:, 0],
+        per_head[:, 1],
+        per_head[:, 2],
     )
 
 

time: 693 us -> 617 us (0.89)
  blocking collectives: 78.3 us -> 0 us
  local copies, waits for them, and re-layouts: 31.2 us -> 39.3 us
    psum x2 -> x0, blocking collectives: 58.5 us -> none  [the longest x1 39.4 us: shards(): head_sums = lax.psum(jnp.stack(per_head, axis=1), ('rep', 'fsdp'))]
    reduce_scatter x4, waiting for transfers between devices: 100 us -> 57 us  [scatter(): return lax.psum_scatter(array, 'fsdp', scatter_dimension=0, tiled=True)]
    all_gather x4, waiting for transfers between devices: 74.4 us -> 101 us  [gather(): return lax.all_gather(array, 'fsdp', axis=0, tiled=True)]
    psum x1, waiting for transfers between devices: 62.5 us -> 84.4 us  [shards(): *wides, outs[0] = lax.psum((*wides, outs[0]), 'rep')]
    all_gather x2 -> x0, blocking collectives: 19.7 us -> none  [gather_layer(): small = lax.all_gather(small, 'fsdp', axis=0).astype(F32)]
    unnamed x11 -> x9, waiting for transfers between devices: 11.2 us -> 0.65 us
  transfers between devices with their start and end apart: 10 -> 9, of which waited for: 6 -> 5; matrix products, arithmetic and copies ran while one was open for 8% -> 10% of each run, Pallas kernels for 20% -> 38%
where the time goes in v2:
time: 617 us; the launch traced here: 613 us
  Pallas kernels  273 us (44%)
  waiting for transfers between devices  243 us (39%)
  local copies, waits for them, and re-layouts  39.3 us (6%)
  matrix products  33.7 us (5%)
  between operations  14.5 us (2%)
  other arithmetic  8.49 us (1%)
    pallas_call x2, Pallas kernels, run_backward(): pl.pallas_call(functools.partial(backward_kernel, (inner, xbc, nstate, pa...  194 us
    all_gather x4, waiting for transfers between devices, gather(): return lax.all_gather(array, 'fsdp', axis=0, tiled=True)  101 us
    psum x1, waiting for transfers between devices, shards(): *wides, outs[0] = lax.psum((*wides, outs[0]), 'rep')  84.4 us
    pallas_call x2, Pallas kernels, run_forward(): pl.pallas_call(functools.partial(forward_kernel, (inner, xbc, nstate, pai...  79 us
    reduce_scatter x4, waiting for transfers between devices, scatter(): return lax.psum_scatter(array, 'fsdp', scatter_dimension=0, tiled=True)  57 us
    dot_general x4, matrix products, dot_tn(): lax.dot_general(left, right, (((0,), (0,)), ((), ())), preferred_element_...  33.7 us
  transfers between devices with their start and end apart: 9, of which 5 were waited for; matrix products, arithmetic and copies ran while one was open for 10% of the time, Pallas kernels for 38%

profile of v2, /device:TPU:0, one launch (start us, length us, event | category | flops | bytes accessed | tf_op | source)
XLA Modules:
  0.0 613.0 jit_solution(9590601916585159843)
XLA Ops:
  7.2 1.4 slice_bitcast_fusion
  10.3 0.8 slice_reduce_fusion.3
  12.9 1.0 concatenate.31
  14.5 1.0 concatenate.33
  15.5 0.8 fusion.10
  20.4 1.1 fusion.1.fold_ref
  21.5 0.8 pad.64.masks_ref
  23.6 34.6 %all-gather.7.cloned.1.call-done.w_ref = bf16[768,3456]{1,0:T(8,128)(2,1)} async-done(((bf16[96,3456]{1,0:T(8,128)(2,1)}), bf16[768,3456]{1,0:T(8,128)(2,1)}) %all-gather.7.cloned.1.call-update) | async-done | bytes 5308432 | tf_op jit(solution)/shard_map/all_gather | solution.py:465
  58.1 1.0 slice_convert_fusion.1
  59.6 42.4 %all-gather.9.cloned.1.call-done.w_ref = bf16[768,3456]{1,0:T(8,128)(2,1)} async-done(((bf16[96,3456]{1,0:T(8,128)(2,1)}), bf16[768,3456]{1,0:T(8,128)(2,1)}) %all-gather.9.cloned.1.call-update) | async-done | bytes 5308432 | tf_op jit(solution)/shard_map/all_gather | solution.py:465
  102.0 1.0 slice_convert_fusion
  109.2 24.4 %all-gather.11.cloned.1.call-done = bf16[1,1536,768]{2,1,0:T(8,128)(2,1)} async-done(((bf16[1,192,768]{2,1,0:T(8,128)(2,1)}), bf16[1,1536,768]{2,1,0:T(8,128)(2,1)}) %all-gather.11.cloned.1.call-update) | async-done | bytes 2359312 | tf_op jit(solution)/shard_map/all_gather | solution.py:465
  133.5 39.4 %layer_forward.2 = (f32[1024,768]{1,0:T(8,128)}, bf16[1024,768]{1,0:T(8,128)(2,1)}, f32[1024,3456]{1,0:T(8,128)}, f32[1024,1536]{1,0:T(8,128)}, bf16[1024,1536]{1,0:T(8,128)(2,1)}, /*index=5*/f32[8,128,1536]{2,1,0:T(8,128)}) custom-call(bf16[1024,768]{1,0:T(8,128)(2,1)} %bitcast.108, f32[1024,16]{1,0:T(8,128)} %pad.64.masks_ref, ...), custom_call_target="tpu_custom_call" | custom-call | flops 60000002048 | bytes 60000000 | tf_op jit(solution)/shard_map/layer_forward/pallas_call | solution.py:342
  173.0 39.6 %layer_forward.3 = (bf16[1024,768]{1,0:T(8,128)(2,1)}, bf16[1024,768]{1,0:T(8,128)(2,1)}, f32[1024,3456]{1,0:T(8,128)}, f32[1024,1536]{1,0:T(8,128)}, bf16[1024,...) custom-call(f32[1024,768]{1,0:T(8,128)} %get-tuple-element.44.h_ref, f32[1024,16]{1,0:T(8,128)} %pad.64.masks_ref, ...), custom_call_target="tpu_custom_call" | custom-call | flops 60000002048 | bytes 60000000 | tf_op jit(solution)/shard_map/layer_forward/pallas_call | solution.py:342
  212.6 6.0 convolution_convert_fusion.3
  218.6 97.3 %layer_backward.2 = (f32[1024,768]{1,0:T(8,128)}, bf16[1024,3456]{1,0:T(8,128)(2,1)}, f32[8,1536]{1,0:T(8,128)}, f32[8,1792]{1,0:T(8,128)}, f32[8,768]{1,0:T(8,1...) custom-call(bf16[1024,768]{1,0:T(8,128)(2,1)} %bitcast.107, f32[1024,768]{1,0:T(8,128)} %get-tuple-element.44.h_ref, ...), custom_call_target="tpu_custom_call" | custom-call | flops 120000004096 | bytes 80000000 | tf_op jit(solution)/shard_map/layer_backward/pallas_call | solution.py:385
  316.0 6.0 convolution_convert_fusion.2
  323.2 0.8 fusion.5
  324.1 0.8 slice_reduce_fusion
  326.2 11.0 %convolution_convert_fusion = bf16[768,3456]{1,0:T(8,128)(2,1)} fusion(bf16[1024,768]{1,0:T(8,128)(2,1)S(1)} %copy-done.13, bf16[1024,3456]{1,0:T(8,128)(2,1)} %get-tuple-element.68), kind=kOutput, calls=%fused_computation | convolution fusion | flops 5438472192 | bytes 13959168 | tf_op jit(solution)/shard_map/dot_general | solution.py:32
  337.2 3.1 dynamic_update_slice.7
  340.4 97.0 %layer_backward.3 = (f32[1024,768]{1,0:T(8,128)}, bf16[1024,3456]{1,0:T(8,128)(2,1)}, f32[8,1536]{1,0:T(8,128)}, f32[8,1792]{1,0:T(8,128)}, f32[8,768]{1,0:T(8,1...) custom-call(f32[1024,768]{1,0:T(8,128)} %get-tuple-element.55.dh_ref, bf16[1024,768]{1,0:T(8,128)(2,1)} %bitcast.109, ...), custom_call_target="tpu_custom_call" | custom-call | flops 120000004096 | bytes 80000000 | tf_op jit(solution)/shard_map/layer_backward/pallas_call | solution.py:385
  437.4 0.8 slice.328
  439.3 0.8 fusion.6
  440.2 0.8 slice_reduce_fusion.1
  442.4 10.7 %convolution_convert_fusion.1 = bf16[768,3456]{1,0:T(8,128)(2,1)} fusion(bf16[1024,768]{1,0:T(8,128)(2,1)S(1)} %copy-done.12, bf16[1024,3456]{1,0:T(8,128)(2,1)} %get-tuple-element.61), kind=kOutput, calls=%fused_computation.1 | convolution fusion | flops 5438472192 | bytes 13959168 | tf_op jit(solution)/shard_map/dot_general | solution.py:32
  453.1 3.1 dynamic_update_slice.6
  456.4 56.9 %reduce-scatter.7.cloned.1.call-done = bf16[96,3456]{1,0:T(8,128)(2,1)} async-done(((bf16[768,3456]{1,0:T(8,128)(2,1)}), bf16[96,3456]{1,0:T(8,128)(2,1)}) %reduce-scatter.7.cloned.1.call-update) | async-done | bytes 663568 | tf_op jit(solution)/shard_map/reduce_scatter | solution.py:469
  513.3 84.4 %all-reduce.18.cloned.1.call-done = (bf16[1,96,3456]{2,1,0:T(8,128)(2,1)}, bf16[1,96,3456]{2,1,0:T(8,128)(2,1)}, bf16[1,192,768]{2,1,0:T(8,128)(2,1)}, bf16[1,192,768]{2,1,0:T(8,128)(2,1)}) async-done(((bf16[1,96,3456]{2,1,0:T(8,128)(2,1)}, bf16[1,96,3456]{2,1,0:T(8,128)(2,1)}, bf16[1,192,768]{2,1,0:T(8,128)(2,1)}, bf16[1,192,768]{2,1,0:T(8,128)(2,1)}), (bf16[1,96,3456]{2,1,0:T(8,128)(2,1)}, ...) | async-done | bytes 1916944 | tf_op jit(solution)/shard_map/psum | solution.py:529
  597.7 1.6 maximum_convert_fusion
  601.5 1.6 slice.278
  605.1 1.1 maximum_convert_fusion.1
  (155 shorter events, 25.1 us)
Async XLA Ops:
  7.2 8.3 %copy-start.2 = (bf16[2,192,768]{2,1,0:T(8,128)(2,1)S(1)}, bf16[2,192,768]{2,1,0:T(8,128)(2,1)}, u32[]{:S(2)}) copy-start(bf16[2,192,768]{2,1,0:T(8,128)(2,1)} %param.17) | copy-start | bytes 1769476
  7.2 51.0 %all-gather.7.cloned.1.call-start = ((), (), s32[]{:S(2)}) async-start(), calls=%async_computation.4 | async-start | bytes 5971968 | tf_op jit(solution)/shard_map/all_gather | solution.py:465
  8.6 8.4 %copy-start.3 = (s32[1,1024]{1,0:T(1,128)S(1)}, s32[1,1024]{1,0:T(1,128)}, u32[]{:S(2)}) copy-start(s32[1,1024]{1,0:T(1,128)} %param.14) | copy-start | bytes 12292
  12.9 6.0 copy-start.7
  13.9 88.1 %all-gather.9.cloned.1.call-start = ((), (), s32[]{:S(2)}) async-start(), calls=%async_computation.5 | async-start | bytes 5971968 | tf_op jit(solution)/shard_map/all_gather | solution.py:465
  14.4 8.0 %copy-start.8 = (f32[2,24]{1,0:T(2,128)S(1)}, f32[2,24]{1,0:T(2,128)}, u32[]{:S(2)}) copy-start(f32[2,24]{1,0:T(2,128)} %param.23) | copy-start | bytes 580
  14.4 7.9 %copy-start.9 = (f32[2,24]{1,0:T(2,128)S(1)}, f32[2,24]{1,0:T(2,128)}, u32[]{:S(2)}) copy-start(f32[2,24]{1,0:T(2,128)} %param.22) | copy-start | bytes 580
  15.5 118.1 %all-gather.11.cloned.1.call-start = ((), (), s32[]{:S(2)}) async-start(), calls=%async_computation.10 | async-start | bytes 2654208 | tf_op jit(solution)/shard_map/all_gather | solution.py:465
  16.4 156.5 %all-gather.13.cloned.1.call-start = ((), (), s32[]{:S(2)}) async-start(), calls=%async_computation.11 | async-start | bytes 2654208 | tf_op jit(solution)/shard_map/all_gather | solution.py:465
  17.0 323.4 %reduce-scatter.5.cloned.1.call-start = ((), (), s32[]{:S(2)}) async-start(), calls=%async_computation.6 | async-start | bytes 2654208 | tf_op jit(solution)/shard_map/reduce_scatter | solution.py:469
  172.9 39.6 %copy-start.10 = (bf16[1,1024,768]{2,1,0:T(8,128)(2,1)S(1)}, bf16[1,1024,768]{2,1,0:T(8,128)(2,1)}, u32[]{:S(2)}) copy-start(bf16[1,1024,768]{2,1,0:T(8,128)(2,1)} %param.25) | copy-start | bytes 4718596
  218.6 237.8 %reduce-scatter.11.cloned.1.call-start = ((), (), s32[]{:S(2)}) async-start(), calls=%async_computation.9 | async-start | bytes 2654208 | tf_op jit(solution)/shard_map/reduce_scatter | solution.py:469
  218.6 97.3 %copy-start.11 = (bf16[1024,1536]{1,0:T(8,128)(2,1)S(1)}, bf16[1024,1536]{1,0:T(8,128)(2,1)}, u32[]{:S(2)}) copy-start(bf16[1024,1536]{1,0:T(8,128)(2,1)} %get-tuple-element.48) | copy-start | bytes 9437188
  315.9 6.1 %copy-start.6 = (f32[8,1792]{1,0:T(8,128)S(1)}, f32[8,1792]{1,0:T(8,128)}, u32[]{:S(2)}) copy-start(f32[8,1792]{1,0:T(8,128)} %get-tuple-element.69) | copy-start | bytes 172036
  315.9 10.3 %copy-start.13 = (bf16[1024,768]{1,0:T(8,128)(2,1)S(1)}, bf16[1024,768]{1,0:T(8,128)(2,1)}, u32[]{:S(2)}) copy-start(bf16[1024,768]{1,0:T(8,128)(2,1)} %get-tuple-element.67) | copy-start | bytes 4718596
  322.0 134.3 %reduce-scatter.9.cloned.1.call-start = ((), (), s32[]{:S(2)}) async-start(), calls=%async_computation.8 | async-start | bytes 5971968 | tf_op jit(solution)/shard_map/reduce_scatter | solution.py:469
  340.4 172.9 %reduce-scatter.7.cloned.1.call-start = ((), (), s32[]{:S(2)}) async-start(), calls=%async_computation.7 | async-start | bytes 5971968 | tf_op jit(solution)/shard_map/reduce_scatter | solution.py:469
  340.4 101.9 %copy-start.12 = (bf16[1024,768]{1,0:T(8,128)(2,1)S(1)}, bf16[1024,768]{1,0:T(8,128)(2,1)}, u32[]{:S(2)}) copy-start(bf16[1024,768]{1,0:T(8,128)(2,1)} %get-tuple-element.60) | copy-start | bytes 4718596
  456.3 141.4 %all-reduce.18.cloned.1.call-start = ((), (), s32[]{:S(2)}) async-start(), calls=%async_computation.12 | async-start | bytes 3833856 | tf_op jit(solution)/shard_map/psum | solution.py:529
  597.7 1.6 copy-start
  597.7 1.7 copy-start.1
  599.4 5.8 copy-start.4
  599.4 5.7 copy-start.5
Sparse Core Ops, SparseCore 0:
  14.0 44.0 all-gather.6
  60.6 41.3 all-gather.8
  104.5 29.0 all-gather.10
  135.3 29.0 all-gather.12
  218.7 42.4 reduce-scatter.4
  322.1 42.4 reduce-scatter.10
  368.0 56.9 reduce-scatter.8
  456.4 56.8 reduce-scatter.6
  515.9 81.6 all-reduce.17
